TPU v7x, 32 devices: a whole 2x2x4 slice. The times are simulated.
32 devices in a mesh: leaf: 8 (over z, y), sub: 4 (over x, core).
Axes of the slice: x: 2, y: 2, z: 4, core: 2. Of those that a mesh axis runs over, the one named last changes fastest.
Arguments:
- fine_mult: bfloat16 [4096, 152], P(('leaf', 'sub')), may hold values from -6 to 6
- m2m_ops: bfloat16 [8, 152, 152], replicated, may hold values from -0.15625 to 0.15625
- m2l_ops: bfloat16 [316, 152, 152], replicated, may hold values from -0.03125 to 0.03125
- check_to_equiv: float32 [152, 152], replicated, may hold values from -0.5 to 0.5
- l2l_ops: bfloat16 [8, 152, 152], replicated, may hold values from -0.5 to 0.5
- send_slots: int32 [32, 32, 64], P(('leaf', 'sub')), may hold values from 0 to 127
- fine_list: int32 [4096, 189], P(('leaf', 'sub')), may hold values from 0 to 2175, as said below
- fine_class: int32 [4096, 189], P(('leaf', 'sub')), may hold values from 0 to 315
- fine_count: int32 [4096], P(('leaf', 'sub')), may hold values from 94 to 189, as said below
- parent_list: int32 [512, 189], P(('leaf', 'sub')), may hold values from 0 to 63
- parent_class: int32 [512, 189], P(('leaf', 'sub')), may hold values from 0 to 315
- parent_count: int32 [512], P(('leaf', 'sub')), may hold values from 94 to 189, as said below
Outputs:
- fine_local: float32 [4096, 152], P(('leaf', 'sub'))
Inputs may be any that keep to these rules, and one draw needn't show every extreme that they name: `fine_list`: codes below 128 name a cell of the target's own device; larger codes name a slot of what another device sends to it. `fine_count`: some cell of every device has a full list. `parent_count`: some parent of every device has a full list.
All inputs are finite; a program needn't handle non-finite values.
Results may differ from a plain program's by a relative error of at most 0.0026.
Values may be sent and summed in bfloat16 or wider, within the bound.
A program may use at most 128 MiB of HBM per device.

v0:
```python
import math

import jax
import jax.numpy as jnp
from jax import lax
from jax.sharding import PartitionSpec as P


def translate(source_table, entry_index, entry_class, entry_count, m2l_ops):
    targets, slot_count = entry_index.shape
    classes, points, _ = m2l_ops.shape
    block_size = math.gcd(targets, 64)

    def translate_block(pieces):
        chosen, kinds, lengths = pieces
        gathered = jnp.take(source_table, chosen.reshape(-1), axis=0, mode="clip")
        gathered = gathered.reshape(block_size, slot_count, points)
        active_slot = lax.broadcasted_iota(jnp.int32, chosen.shape, 1) < lengths[:, None]
        class_range = lax.broadcasted_iota(jnp.int32, (1, classes, 1), 1)
        onehot = ((kinds[:, None, :] == class_range) & active_slot[:, None, :]).astype(jnp.bfloat16)
        summed = jnp.einsum("tcl,tlq->tcq", onehot, gathered, preferred_element_type=jnp.float32)
        summed = summed.astype(jnp.bfloat16)
        return jnp.einsum("tcq,cqj->tj", summed, m2l_ops, preferred_element_type=jnp.float32)

    results = lax.map(
        translate_block,
        (
            entry_index.reshape(-1, block_size, slot_count),
            entry_class.reshape(-1, block_size, slot_count),
            entry_count.reshape(-1, block_size),
        ),
    )
    return results.reshape(targets, points)


def body(
    fine_mult,
    m2m_ops,
    m2l_ops,
    check_to_equiv,
    l2l_ops,
    send_slots,
    fine_list,
    fine_class,
    fine_count,
    parent_list,
    parent_class,
    parent_count,
):
    cell_total, points = fine_mult.shape
    peer_count = send_slots.shape[1]
    capacity = send_slots.shape[2]
    outgoing = jnp.take(fine_mult, send_slots[0].reshape(-1), axis=0, mode="clip")
    outgoing = outgoing.reshape(peer_count, capacity, points)
    received = lax.all_to_all(outgoing, ("leaf", "sub"), split_axis=0, concat_axis=0, tiled=True)
    received = received.reshape(peer_count * capacity, points)
    source_table = jnp.concatenate([fine_mult, received], axis=0)
    fine_check = translate(source_table, fine_list, fine_class, fine_count, m2l_ops)
    children = fine_mult.reshape(cell_total // 8, 8, points)
    parent_mult = jnp.einsum(
        "pkq,kqr->pr", children, m2m_ops, preferred_element_type=jnp.float32
    ).astype(jnp.bfloat16)
    block_parents = lax.all_gather(parent_mult, "sub", axis=0, tiled=True)
    parent_check = 0.5 * translate(block_parents, parent_list, parent_class, parent_count, m2l_ops)
    parent_local = jnp.dot(
        parent_check,
        check_to_equiv,
        precision=lax.Precision.HIGHEST,
        preferred_element_type=jnp.float32,
    ).astype(jnp.bfloat16)
    downward = jnp.einsum("pq,kqr->pkr", parent_local, l2l_ops, preferred_element_type=jnp.float32)
    return fine_check + downward.reshape(cell_total, points)


def solution(mesh):
    in_specs = (
        P(("leaf", "sub"), None),
        P(),
        P(),
        P(),
        P(),
        P(("leaf", "sub"), None, None),
        P(("leaf", "sub"), None),
        P(("leaf", "sub"), None),
        P(("leaf", "sub")),
        P(("leaf", "sub"), None),
        P(("leaf", "sub"), None),
        P(("leaf", "sub")),
    )
    out_specs = P(("leaf", "sub"), None)
    return jax.shard_map(body, mesh=mesh, in_specs=in_specs, out_specs=out_specs, check_vma=False)
```

profile of v0, /device:TPU:0, one launch (start us, length us, event | category | flops | bytes accessed | tf_op | source)
XLA Modules:
  0.0 208.9 jit_solution(3249571202884585247)
XLA Ops:
  0.0 0.0 copy-start
  0.0 0.9 reshape.108
  0.9 0.9 copy.52
  1.7 0.0 copy-start.12
  1.8 0.0 copy-start.10
  1.8 0.0 copy-start.9
  1.8 0.0 copy-start.3
  1.8 0.0 copy-start.7
  1.8 0.0 copy-start.8
  1.8 9.0 %gather_fusion.1 = bf16[2048,152]{1,0:T(8,128)(2,1)} fusion(bf16[128,152]{1,0:T(8,128)(2,1)S(1)} %copy.52, s32[2048]{0:T(1024)S(1)} %broadcast_clamp_fusion), kind=kCustom, calls=%fused_computation.1 | custom fusion | bytes 1253376 | tf_op jit(solution)/shard_map/jit(_take)/gather | solution.py:53
  10.9 7.3 %all-to-all-start = ((bf16[32,64,152]{2,1,0:T(8,128)(2,1)}), bf16[32,64,152]{2,1,0:T(8,128)(2,1)S(1)}, u32[]{:S(2)}, u32[]{:S(2)}) async-start(bf16[32,64,152]{2,1,0:T(8,128)(2,1)} %bitcast.6), calls=%async_computation | async-start | bytes 2097152 | tf_op jit(solution)/shard_map/all_to_all | solution.py:55
  18.2 0.0 copy-done.12
  18.2 0.1 reshape.90
  18.3 0.0 copy-done.10
  18.3 0.1 iota_compare_fusion.3
  18.3 0.0 copy-done.9
  18.3 0.1 reshape.116
  18.5 0.0 copy-done.3
  18.5 0.2 fusion.31
  18.7 7.0 %all_gather.3 = bf16[64,152]{1,0:T(8,128)(2,1)S(1)} all-gather(bf16[16,152]{1,0:T(8,128)(2,1)S(1)} %fusion.31), channel_id=1, replica_groups=mesh['leaf'=8,'sub'=4] {'sub'}, dimensions={0}, use_global_device_ids=true | all-gather | bytes 24320 | tf_op jit(solution)/shard_map/all_gather | solution.py:63
  25.7 0.0 copy-done.7
  25.7 0.1 copy.50
  25.8 0.0 copy-done.8
  25.8 0.8 copy.49
  26.5 0.0 copy-start.11
  26.5 11.3 %gather_fusion.2 = bf16[3024,152]{1,0:T(8,128)(2,1)S(1)} fusion(bf16[64,152]{1,0:T(8,128)(2,1)S(1)} %all_gather.3, s32[3072]{0:T(1024)S(1)} %pad_clamp_fusion.1), kind=kCustom, calls=%fused_computation.2 | custom fusion | bytes 1850688 | tf_op jit(solution)/shard_map/while/body/eval_jaxpr/jit(_take)/gather | solution.py:16
  37.8 1.4 reshape.130
  39.2 0.0 copy-done.11
  39.3 4.4 %fusion.22 = bf16[16,316,152]{1,2,0:T(8,128)(2,1)} fusion(bf16[16,189,152]{2,1,0:T(8,128)(2,1)} %reshape.130, s32[16,189]{1,0:T(8,128)S(1)} %copy-done.11, pred[16,189]{1,0:T(8,128)(4,1)S(1)} %iota_compare_fusion.3), kind=kOutput, calls=%fused_computation.25 | convolution fusion | flops 293177216 | bytes 2471440 | tf_op jit(solution)/shard_map/while/body/eval_jaxpr/tcl,tlq->tcq/dot_general | solution.py:21
  43.7 0.0 copy-start.5
  43.7 0.0 copy-start.2
  43.7 0.0 copy-start.6
  43.7 11.3 %fusion.28 = f32[16,152]{1,0:T(8,128)S(1)} fusion(bf16[316,152,152]{0,2,1:T(8,128)(2,1)} %param.16, bf16[16,316,152]{1,2,0:T(8,128)(2,1)} %fusion.22), kind=kOutput, calls=%fused_computation.28 | convolution fusion | flops 233630080 | bytes 16148480 | tf_op jit(solution)/shard_map/while/body/eval_jaxpr/tcq,cqj->tj/dot_general | solution.py:23
  55.0 0.0 copy-done.5
  55.0 0.2 fusion.32
  55.2 0.0 copy-done
  55.2 0.2 fusion.34
  55.4 0.1 copy.87
  55.5 0.7 copy.61
  56.2 0.0 all-to-all-done
  56.2 0.0 copy-start.1
  56.2 1.0 copy-done.1
  57.2 1.4 pad_maximum_fusion
  58.6 0.0 copy-done.2
  58.6 0.0 copy-done.6
  58.6 0.0 copy-start.4
  58.7 149.4 %while.2 = (s32[]{:T(128)}, f32[2,64,152]{2,1,0:T(8,128)S(1)}, s32[2,64,189]{2,1,0:T(8,128)S(1)}, s32[2,64]{1,0:T(2,128)S(1)}, s32[2,64,189]{2,1,0:T(8,128)S(1)}...) while((s32[]{:T(128)}, f32[2,64,152]{2,1,0:T(8,128)S(1)}, ...), condition=%wide.region_1.2_spmd, body=%wide.region_0.1_spmd.sunk | while | flops 2107243904 | bytes 53600488 | solution.py:25
  58.9 0.2 reshape.137
  59.1 0.1 copy.93
  59.2 7.8 %fusion.57 = pred[64,316,189]{1,0,2:T(32,128)(4,1)} fusion(s32[64,189]{0,1:T(8,128)S(1)} %bitcast.47, pred[64,189]{0,1:T(8,128)(4,1)S(1)} %iota_compare_fusion.5), kind=kLoop, calls=%fused_computation.6.clone.1 | loop fusion | flops 7644672 | bytes 3882816 | tf_op jit(solution)/shard_map/while/body/eval_jaxpr/and | solution.py:20
  67.1 34.7 %gather_fusion = bf16[12096,152]{1,0:T(8,128)(2,1)} fusion(bf16[2176,152]{1,0:T(8,128)(2,1)S(1)} %get-tuple-element.155, s32[12288]{0:T(1024)S(1)} %pad_clamp_fusion.3), kind=kCustom, calls=%fused_computation.clone.1 | custom fusion | bytes 7402752 | tf_op jit(solution)/shard_map/while/body/eval_jaxpr/jit(_take)/gather | solution.py:16
  101.8 8.4 %reshape.138 = bf16[64,189,152]{2,1,0:T(8,128)(2,1)} reshape(bf16[12096,152]{1,0:T(8,128)(2,1)} %gather_fusion) | data formatting | bytes 7354368 | tf_op jit(solution)/shard_map/while/body/eval_jaxpr/reshape | solution.py:17
  110.2 11.2 %fusion.58 = bf16[64,316,152]{1,2,0:T(8,128)(2,1)} fusion(bf16[64,189,152]{2,1,0:T(8,128)(2,1)} %reshape.138, pred[64,316,189]{1,0,2:T(32,128)(4,1)} %fusion.57), kind=kOutput, calls=%fused_computation.9.clone.1 | convolution fusion | flops 1165064192 | bytes 13647616 | tf_op jit(solution)/shard_map/while/body/eval_jaxpr/tcl,tlq->tcq/dot_general | solution.py:21
  121.4 12.1 %fusion.59 = f32[2,64,152]{2,1,0:T(8,128)S(1)} fusion(f32[2,64,152]{2,1,0:T(8,128)S(1)} %get-tuple-element.143, s32[]{:T(128)S(6)} %copy.97, bf16[316,152,152]{0,2,1:T(8,128)(2,1)} %get-tuple-element.156, bf16[64,316,152]{1,2,0:T(8,128)(2,1)} %fusion.58), kind=kOutput, calls=%fused_computation.11.clone.1 | convolution fusion | flops 934510592 | bytes 20815364 | tf_op jit(solution)/shard_map/while/body/eval_jaxpr/tcq,cqj->tj/dot_general | solution.py:23
  133.6 0.2 reshape.137
  133.8 0.1 copy.93
  133.9 7.8 %fusion.57 = pred[64,316,189]{1,0,2:T(32,128)(4,1)} fusion(s32[64,189]{0,1:T(8,128)S(1)} %bitcast.47, pred[64,189]{0,1:T(8,128)(4,1)S(1)} %iota_compare_fusion.5), kind=kLoop, calls=%fused_computation.6.clone.1 | loop fusion | flops 7644672 | bytes 3882816 | tf_op jit(solution)/shard_map/while/body/eval_jaxpr/and | solution.py:20
  141.7 34.7 %gather_fusion = bf16[12096,152]{1,0:T(8,128)(2,1)} fusion(bf16[2176,152]{1,0:T(8,128)(2,1)S(1)} %get-tuple-element.155, s32[12288]{0:T(1024)S(1)} %pad_clamp_fusion.3), kind=kCustom, calls=%fused_computation.clone.1 | custom fusion | bytes 7402752 | tf_op jit(solution)/shard_map/while/body/eval_jaxpr/jit(_take)/gather | solution.py:16
  176.4 8.4 %reshape.138 = bf16[64,189,152]{2,1,0:T(8,128)(2,1)} reshape(bf16[12096,152]{1,0:T(8,128)(2,1)} %gather_fusion) | data formatting | bytes 7354368 | tf_op jit(solution)/shard_map/while/body/eval_jaxpr/reshape | solution.py:17
  184.8 11.2 %fusion.58 = bf16[64,316,152]{1,2,0:T(8,128)(2,1)} fusion(bf16[64,189,152]{2,1,0:T(8,128)(2,1)} %reshape.138, pred[64,316,189]{1,0,2:T(32,128)(4,1)} %fusion.57), kind=kOutput, calls=%fused_computation.9.clone.1 | convolution fusion | flops 1165064192 | bytes 13647616 | tf_op jit(solution)/shard_map/while/body/eval_jaxpr/tcl,tlq->tcq/dot_general | solution.py:21
  196.0 12.1 %fusion.59 = f32[2,64,152]{2,1,0:T(8,128)S(1)} fusion(f32[2,64,152]{2,1,0:T(8,128)S(1)} %get-tuple-element.143, s32[]{:T(128)S(6)} %copy.97, bf16[316,152,152]{0,2,1:T(8,128)(2,1)} %get-tuple-element.156, bf16[64,316,152]{1,2,0:T(8,128)(2,1)} %fusion.58), kind=kOutput, calls=%fused_computation.11.clone.1 | convolution fusion | flops 934510592 | bytes 20815364 | tf_op jit(solution)/shard_map/while/body/eval_jaxpr/tcq,cqj->tj/dot_general | solution.py:23
  208.1 0.1 copy.64
  208.2 0.0 copy-done.4
  208.2 0.6 add.8
  (11 shorter events, 0.1 us)
Async XLA Ops:
  0.0 55.2 %copy-start = (bf16[8,152,152]{2,1,0:T(8,128)(2,1)S(1)}, bf16[8,152,152]{2,1,0:T(8,128)(2,1)}, u32[]{:S(2)}) copy-start(bf16[8,152,152]{2,1,0:T(8,128)(2,1)} %param.18) | copy-start | bytes 1108996
  1.7 16.4 %copy-start.12 = (s32[128]{0:T(128)S(1)}, s32[128]{0:T(128)}, u32[]{:S(2)}) copy-start(s32[128]{0:T(128)} %param.22) | copy-start | bytes 1540
  1.8 16.5 %copy-start.10 = (s32[16]{0:T(128)S(1)}, s32[16]{0:T(128)}, u32[]{:S(2)}) copy-start(s32[16]{0:T(128)} %param.25) | copy-start | bytes 196
  1.8 16.6 %copy-start.9 = (s32[16,189]{1,0:T(8,128)S(1)}, s32[16,189]{1,0:T(8,128)}, u32[]{:S(2)}) copy-start(s32[16,189]{1,0:T(8,128)} %param.23) | copy-start | bytes 36292
  1.8 16.7 %copy-start.3 = (bf16[8,152,152]{2,1,0:T(8,128)(2,1)S(1)}, bf16[8,152,152]{2,1,0:T(8,128)(2,1)}, u32[]{:S(2)}) copy-start(bf16[8,152,152]{2,1,0:T(8,128)(2,1)} %param.15) | copy-start | bytes 1108996
  1.8 23.9 %copy-start.7 = (s32[128,189]{0,1:T(8,128)S(1)}, s32[128,189]{0,1:T(8,128)}, u32[]{:S(2)}) copy-start(s32[128,189]{0,1:T(8,128)} %param.20) | copy-start | bytes 290308
  1.8 24.0 %copy-start.8 = (s32[128,189]{0,1:T(8,128)S(1)}, s32[128,189]{0,1:T(8,128)}, u32[]{:S(2)}) copy-start(s32[128,189]{0,1:T(8,128)} %param.21) | copy-start | bytes 290308
  10.9 45.4 %all-to-all-start = ((bf16[32,64,152]{2,1,0:T(8,128)(2,1)}), bf16[32,64,152]{2,1,0:T(8,128)(2,1)S(1)}, u32[]{:S(2)}, u32[]{:S(2)}) async-start(bf16[32,64,152]{2,1,0:T(8,128)(2,1)} %bitcast.6), calls=%async_computation | async-start | bytes 2097152 | tf_op jit(solution)/shard_map/all_to_all | solution.py:55
  26.5 12.7 %copy-start.11 = (s32[16,189]{1,0:T(8,128)S(1)}, s32[16,189]{1,0:T(8,128)}, u32[]{:S(2)}) copy-start(s32[16,189]{1,0:T(8,128)} %param.24) | copy-start | bytes 36292
  43.7 11.3 %copy-start.5 = (f32[152,152]{1,0:T(8,128)S(1)}, f32[152,152]{1,0:T(8,128)}, u32[]{:S(2)}) copy-start(f32[152,152]{1,0:T(8,128)} %param.17) | copy-start | bytes 277252
  43.7 14.9 %copy-start.2 = (s32[128,189]{1,0:T(8,128)S(1)}, s32[128,189]{1,0:T(8,128)}, u32[]{:S(2)}) copy-start(s32[128,189]{1,0:T(8,128)} %copy.49) | copy-start | bytes 290308
  43.7 15.0 %copy-start.6 = (f32[2,64,152]{2,1,0:T(8,128)S(1)}, f32[2,64,152]{2,1,0:T(8,128)}, u32[]{:S(2)}) copy-start(f32[2,64,152]{2,1,0:T(8,128)} %custom-call.6) | copy-start | bytes 233476
  56.2 1.0 copy-start.1
  58.6 149.6 %copy-start.4 = (f32[128,152]{0,1:T(8,128)S(1)}, f32[128,152]{0,1:T(8,128)}, u32[]{:S(2)}) copy-start(f32[128,152]{0,1:T(8,128)} %copy.61) | copy-start | bytes 233476
where the time goes:
time: 212 us; the launch traced here: 209 us
  local copies, waits for them, and re-layouts  113 us (53%)
  matrix products  62.9 us (30%)
  other arithmetic  17.9 us (8%)
  starting transfers between devices  7.3 us (3%)
  blocking collectives  6.95 us (3%)
    gather x3, local copies, waits for them, and re-layouts, translate_block(): gathered = jnp.take(source_table, chosen.reshape(-1), axis=0, mode='clip')  80.7 us
    dot_general x3, matrix products, translate_block(): jnp.einsum('tcq,cqj->tj', summed, m2l_ops, preferred_element_type=jnp.flo...  35.5 us
    dot_general x3, matrix products, translate_block(): jnp.einsum('tcl,tlq->tcq', onehot, gathered, preferred_element_type=jnp.f...  26.8 us
    reshape x3, local copies, waits for them, and re-layouts, translate_block(): gathered = gathered.reshape(block_size, slot_count, points)  18.3 us
    and x2, other arithmetic, translate_block(): (kinds[:, None, :] == class_range) & active_slot[:, None, :]  15.7 us
    gather x1, local copies, waits for them, and re-layouts, body(): jnp.take(fine_mult, send_slots[0].reshape(-1), axis=0, mode='clip')  9.04 us
    all_to_all x1, starting transfers between devices, body(): lax.all_to_all(outgoing, ('leaf', 'sub'), split_axis=0, concat_axis=0, ti...  7.3 us
    all_gather x1, blocking collectives, body(): block_parents = lax.all_gather(parent_mult, 'sub', axis=0, tiled=True)  6.95 us
  transfers between devices with their start and end apart: 1, of which 0 were waited for; matrix products, arithmetic and copies ran while one was open for 15% of the time, Pallas kernels for 0%

commit v1 on v0

v1 whole, which is shorter than its diff:
```python
import functools

import jax
import jax.numpy as jnp
from jax import lax
from jax.experimental import pallas as pl
from jax.experimental.pallas import tpu as pltpu
from jax.sharding import PartitionSpec as P

GROUP = 16
CHUNK = 4
BUFFERS = 8


def translate_kernel(targets, slots, classes, points, row_ref, sum_ref, steps_ref, table_ref, ops_ref, out_ref,
                     sums, ops, sems):
    chunks = classes // CHUNK

    def fetch(chunk, buffer):
        return pltpu.make_async_copy(ops_ref.at[pl.ds(chunk * CHUNK, CHUNK)], ops.at[buffer], sems.at[buffer])

    for b in range(BUFFERS):
        fetch(b, b).start()

    flat = sums.reshape(sums.shape[0] * 2, 128)

    def clear(i, _):
        flat[pl.ds(i * 2 * targets, 2 * targets), :] = jnp.zeros((2 * targets, 128), jnp.float32)
        return 0

    lax.fori_loop(0, classes, clear, 0)

    def group(g, _):
        def step(e, _):
            base = (g * slots + e) * GROUP
            places = [sum_ref[base + i] for i in range(GROUP)]
            rows = [row_ref[base + i] for i in range(GROUP)]
            values = [sums[places[i]] + table_ref[rows[i]] for i in range(GROUP)]
            for i in range(GROUP):
                sums[places[i]] = values[i]
            return 0

        lax.fori_loop(0, steps_ref[g], step, 0)
        return 0

    lax.fori_loop(0, targets // GROUP, group, 0)

    out_ref[...] = jnp.zeros_like(out_ref)

    def multiply(chunk, _):
        buffer = lax.rem(chunk, BUFFERS)
        fetch(chunk, buffer).wait()
        total = out_ref[...]
        for i in range(CHUNK):
            start = (chunk * CHUNK + i) * 2 * targets
            low = flat[pl.ds(start, targets, stride=2), :]
            high = flat[pl.ds(start + 1, targets, stride=2), :]
            left = jnp.concatenate([low.astype(jnp.bfloat16), high.astype(jnp.bfloat16)], axis=1)[:, :points]
            total += jnp.dot(left, ops[buffer, i], preferred_element_type=jnp.float32)
        out_ref[...] = total

        @pl.when(chunk + BUFFERS < chunks)
        def _():
            fetch(chunk + BUFFERS, buffer).start()

        return 0

    lax.fori_loop(0, chunks, multiply, 0)


def translate(table, entry_row, entry_class, entry_count, m2l_ops):
    targets, slots = entry_row.shape
    classes, points, _ = m2l_ops.shape
    groups = targets // GROUP
    live = lax.broadcasted_iota(jnp.int32, entry_row.shape, 1) < entry_count[:, None]
    target = lax.broadcasted_iota(jnp.int32, entry_row.shape, 0)
    places = jnp.where(live, entry_class, classes) * targets + target

    def arrange(x):
        return x.reshape(groups, GROUP, slots).transpose(0, 2, 1).reshape(-1)

    steps = jnp.max(entry_count.reshape(groups, GROUP), axis=1)
    smem = pl.BlockSpec(memory_space=pltpu.SMEM)
    vmem = pl.BlockSpec(memory_space=pltpu.VMEM)
    return pl.pallas_call(
        functools.partial(translate_kernel, targets, slots, classes, points),
        out_shape=jax.ShapeDtypeStruct((targets, points), jnp.float32),
        in_specs=[smem, smem, smem, vmem, pl.BlockSpec(memory_space=pl.ANY)],
        out_specs=vmem,
        scratch_shapes=[
            pltpu.VMEM(((classes + 1) * targets, 2, 128), jnp.float32),
            pltpu.VMEM((BUFFERS, CHUNK, points, points), jnp.bfloat16),
            pltpu.SemaphoreType.DMA((BUFFERS,)),
        ],
        compiler_params=pltpu.CompilerParams(vmem_limit_bytes=62 * 2**20),
    )(arrange(entry_row), arrange(places), steps, table, m2l_ops)


def body(
    fine_mult,
    m2m_ops,
    m2l_ops,
    check_to_equiv,
    l2l_ops,
    send_slots,
    fine_list,
    fine_class,
    fine_count,
    parent_list,
    parent_class,
    parent_count,
):
    cell_total, points = fine_mult.shape
    peer_count = send_slots.shape[1]
    capacity = send_slots.shape[2]
    outgoing = jnp.take(fine_mult, send_slots[0].reshape(-1), axis=0, mode="clip")
    outgoing = outgoing.reshape(peer_count, capacity, points)
    received = lax.all_to_all(outgoing, ("leaf", "sub"), split_axis=0, concat_axis=0, tiled=True)
    received = received.reshape(peer_count * capacity, points)
    children = fine_mult.reshape(cell_total // 8, 8, points)
    parent_mult = jnp.einsum(
        "pkq,kqr->pr", children, m2m_ops, preferred_element_type=jnp.float32
    ).astype(jnp.bfloat16)
    block_parents = lax.all_gather(parent_mult, "sub", axis=0, tiled=True)
    table = jnp.concatenate([fine_mult, received, block_parents], axis=0).astype(jnp.float32)
    table = jnp.pad(table, ((0, 0), (0, 256 - points))).reshape(-1, 2, 128)
    parent_first = cell_total + peer_count * capacity
    check = translate(
        table,
        jnp.concatenate([fine_list, parent_list + parent_first], axis=0),
        jnp.concatenate([fine_class, parent_class], axis=0),
        jnp.concatenate([fine_count, parent_count], axis=0),
        m2l_ops,
    )
    fine_check, parent_check = check[:cell_total], 0.5 * check[cell_total:]
    parent_local = jnp.dot(
        parent_check,
        check_to_equiv,
        precision=lax.Precision.HIGHEST,
        preferred_element_type=jnp.float32,
    ).astype(jnp.bfloat16)
    downward = jnp.einsum("pq,kqr->pkr", parent_local, l2l_ops, preferred_element_type=jnp.float32)
    return fine_check + downward.reshape(cell_total, points)


def solution(mesh):
    in_specs = (
        P(("leaf", "sub"), None),
        P(),
        P(),
        P(),
        P(),
        P(("leaf", "sub"), None, None),
        P(("leaf", "sub"), None),
        P(("leaf", "sub"), None),
        P(("leaf", "sub")),
        P(("leaf", "sub"), None),
        P(("leaf", "sub"), None),
        P(("leaf", "sub")),
    )
    out_specs = P(("leaf", "sub"), None)
    return jax.shard_map(body, mesh=mesh, in_specs=in_specs, out_specs=out_specs, check_vma=False)
```

time: 212 us -> 205 us (0.967)
  Pallas kernels: 0 us -> 131 us
  matrix products: 62.9 us -> 1.31 us
  local copies, waits for them, and re-layouts: 113 us -> 54.7 us
  other arithmetic: 17.9 us -> 3.26 us
    pallas_call x0 -> x1, Pallas kernels: none -> 131 us  [translate(): pl.pallas_call(functools.partial(translate_kernel, targets, slots, classe...]
    gather x3 -> x0, local copies, waits for them, and re-layouts: 80.7 us -> none  [translate_block(): gathered = jnp.take(source_table, chosen.reshape(-1), axis=0, mode='clip')]
    dot_general x6 -> x0, matrix products: 62.3 us -> none  [the longest x3 35.5 us: translate_block(): jnp.einsum('tcq,cqj->tj', summed, m2l_ops, preferred_element_type=jnp.flo...]
    unnamed x29 -> x24, local copies, waits for them, and re-layouts: 2.76 us -> 39.3 us
    and x2 -> x0, other arithmetic: 15.7 us -> none  [translate_block(): (kinds[:, None, :] == class_range) & active_slot[:, None, :]]
    reshape x6 -> x3, local copies, waits for them, and re-layouts: 19.2 us -> 4.07 us  [the longest x1 2.23 us: body(): table = jnp.pad(table, ((0, 0), (0, 256 - points))).reshape(-1, 2, 128)]
  transfers between devices with their start and end apart: 1 -> 1, of which waited for: 0 -> 0; matrix products, arithmetic and copies ran while one was open for 15% -> 20% of each run, Pallas kernels for 0% -> 0%
where the time goes in v1:
time: 205 us; the launch traced here: 203 us
  Pallas kernels  131 us (64%)
  local copies, waits for them, and re-layouts  54.7 us (27%)
  starting transfers between devices  7.3 us (4%)
  blocking collectives  5.19 us (3%)
  other arithmetic  3.26 us (2%)
    pallas_call x1, Pallas kernels, translate(): pl.pallas_call(functools.partial(translate_kernel, targets, slots, classe...  131 us
    unnamed x24, local copies, waits for them, and re-layouts  39.3 us
    gather x1, local copies, waits for them, and re-layouts, body(): jnp.take(fine_mult, send_slots[0].reshape(-1), axis=0, mode='clip')  9.05 us
    all_to_all x1, starting transfers between devices, body(): lax.all_to_all(outgoing, ('leaf', 'sub'), split_axis=0, concat_axis=0, ti...  7.3 us
    all_gather x1, blocking collectives, body(): block_parents = lax.all_gather(parent_mult, 'sub', axis=0, tiled=True)  5.19 us
  transfers between devices with their start and end apart: 1, of which 0 were waited for; matrix products, arithmetic and copies ran while one was open for 20% of the time, Pallas kernels for 0%

profile of v1, /device:TPU:0, one launch (start us, length us, event | category | flops | bytes accessed | tf_op | source)
XLA Modules:
  0.0 203.0 jit_solution(16616311524417988680)
XLA Ops:
  0.0 0.0 copy-start
  0.0 0.9 reshape.59
  0.9 0.9 copy.28
  1.7 0.0 copy-start.8
  1.8 0.0 copy-start.9
  1.8 0.0 copy-start.4
  1.8 9.0 %gather_fusion = bf16[2048,152]{1,0:T(8,128)(2,1)} fusion(bf16[128,152]{1,0:T(8,128)(2,1)S(1)} %copy.28, s32[2048]{0:T(1024)S(1)} %broadcast_clamp_fusion), kind=kCustom, calls=%fused_computation | custom fusion | bytes 1253376 | tf_op jit(solution)/shard_map/jit(_take)/gather | solution.py:116
  10.8 0.0 copy-start.5
  10.8 0.0 copy-start.6
  10.8 0.0 copy-start.7
  10.8 7.3 %all-to-all-start = ((bf16[32,64,152]{2,1,0:T(8,128)(2,1)}), bf16[32,64,152]{2,1,0:T(8,128)(2,1)S(1)}, u32[]{:S(2)}, u32[]{:S(2)}) async-start(bf16[32,64,152]{2,1,0:T(8,128)(2,1)} %bitcast.4), calls=%async_computation | async-start | bytes 2097152 | tf_op jit(solution)/shard_map/all_to_all | solution.py:118
  18.1 0.0 copy-done.8
  18.1 0.0 copy-done.9
  18.2 0.1 lt.11
  18.2 0.0 copy-done.4
  18.2 0.1 copy.21
  18.4 0.0 copy-done.5
  18.4 0.1 copy.23
  18.5 0.6 reduce_max.9.steps_ref
  19.1 0.0 copy-done.6
  19.1 0.1 add_bitcast_fusion
  19.2 0.3 copy.24
  19.5 0.9 reshape.48.sum_ref
  20.5 0.0 copy-done.7
  20.5 0.3 copy.22
  20.8 0.9 reshape.47.row_ref
  21.7 0.0 copy-start.2
  21.7 37.2 %copy.29.ops_ref = bf16[316,152,152]{2,1,0:T(8,128)(2,1)} copy(bf16[316,152,152]{0,2,1:T(8,128)(2,1)} %param.14) | data formatting | bytes 29203456 | tf_op args[2]
  58.9 0.0 copy-done.2
  58.9 0.2 fusion.6
  59.1 5.2 %all_gather.3 = bf16[64,152]{1,0:T(8,128)(2,1)S(1)} all-gather(bf16[16,152]{1,0:T(8,128)(2,1)S(1)} %fusion.6), channel_id=1, replica_groups=mesh['leaf'=8,'sub'=4] {'sub'}, dimensions={0}, use_global_device_ids=true | all-gather | bytes 24320 | tf_op jit(solution)/shard_map/all_gather | solution.py:124
  64.3 0.0 all-to-all-done
  64.3 0.0 copy-start.1
  64.3 1.1 copy-done.1
  65.4 1.5 fusion.5
  66.9 2.2 %reshape.56.table_ref = f32[2240,2,128]{2,1,0:T(2,128)} reshape(f32[2240,256]{1,0:T(8,128)S(1)} %fusion.5) | data formatting | bytes 4587520 | tf_op jit(solution)/shard_map/reshape | solution.py:126
  69.1 0.0 copy-start.3
  69.1 131.0 %shard_map.118 = f32[144,152]{1,0:T(8,128)} custom-call(s32[27216]{0:T(1024)} %reshape.47.row_ref, s32[27216]{0:T(1024)} %reshape.48.sum_ref, s32[9]{0:T(128)} %reduce_max.9.steps_ref, f32[2240,2,128]{2,1,0:T(2,128)} %reshape.56.table_ref, bf16[316,152,152]{2,1,0:T(8,128)(2,1)} %copy.29.ops_ref), custom_call_target="tpu_custom_call" | custom-call | tf_op jit(solution)/shard_map/pallas_call | solution.py:85
  200.1 0.0 copy-done.3
  200.1 0.9 fusion.7
  201.0 0.0 copy-done
  201.0 0.2 fusion.11
  201.2 1.0 slice_add_fusion
  202.2 0.7 copy.31
  (6 shorter events, 0.0 us)
Async XLA Ops:
  0.0 201.0 %copy-start = (bf16[8,152,152]{2,1,0:T(8,128)(2,1)S(1)}, bf16[8,152,152]{2,1,0:T(8,128)(2,1)}, u32[]{:S(2)}) copy-start(bf16[8,152,152]{2,1,0:T(8,128)(2,1)} %param.16) | copy-start | bytes 1108996
  1.7 16.4 %copy-start.8 = (s32[16]{0:T(128)S(1)}, s32[16]{0:T(128)}, u32[]{:S(2)}) copy-start(s32[16]{0:T(128)} %param.23) | copy-start | bytes 196
  1.8 16.4 %copy-start.9 = (s32[128]{0:T(128)S(1)}, s32[128]{0:T(128)}, u32[]{:S(2)}) copy-start(s32[128]{0:T(128)} %param.20) | copy-start | bytes 1540
  1.8 16.5 %copy-start.4 = (s32[128,189]{0,1:T(8,128)S(1)}, s32[128,189]{0,1:T(8,128)}, u32[]{:S(2)}) copy-start(s32[128,189]{0,1:T(8,128)} %param.18) | copy-start | bytes 290308
  10.8 7.5 %copy-start.5 = (s32[128,189]{0,1:T(8,128)S(1)}, s32[128,189]{0,1:T(8,128)}, u32[]{:S(2)}) copy-start(s32[128,189]{0,1:T(8,128)} %param.19) | copy-start | bytes 290308
  10.8 8.3 %copy-start.6 = (s32[16,189]{1,0:T(8,128)S(1)}, s32[16,189]{1,0:T(8,128)}, u32[]{:S(2)}) copy-start(s32[16,189]{1,0:T(8,128)} %param.22) | copy-start | bytes 36292
  10.8 9.6 %copy-start.7 = (s32[16,189]{1,0:T(8,128)S(1)}, s32[16,189]{1,0:T(8,128)}, u32[]{:S(2)}) copy-start(s32[16,189]{1,0:T(8,128)} %param.21) | copy-start | bytes 36292
  10.8 53.5 %all-to-all-start = ((bf16[32,64,152]{2,1,0:T(8,128)(2,1)}), bf16[32,64,152]{2,1,0:T(8,128)(2,1)S(1)}, u32[]{:S(2)}, u32[]{:S(2)}) async-start(bf16[32,64,152]{2,1,0:T(8,128)(2,1)} %bitcast.4), calls=%async_computation | async-start | bytes 2097152 | tf_op jit(solution)/shard_map/all_to_all | solution.py:118
  21.7 37.2 %copy-start.2 = (bf16[8,152,152]{2,1,0:T(8,128)(2,1)S(1)}, bf16[8,152,152]{2,1,0:T(8,128)(2,1)}, u32[]{:S(2)}) copy-start(bf16[8,152,152]{2,1,0:T(8,128)(2,1)} %param.13) | copy-start | bytes 1108996
  64.3 1.1 copy-start.1
  69.1 131.0 %copy-start.3 = (f32[152,152]{1,0:T(8,128)S(1)}, f32[152,152]{1,0:T(8,128)}, u32[]{:S(2)}) copy-start(f32[152,152]{1,0:T(8,128)} %param.15) | copy-start | bytes 277252

commit v2 on v0

v2 whole, which is shorter than its diff:
```python
import functools

import jax
import jax.numpy as jnp
from jax import lax
from jax.experimental import pallas as pl
from jax.experimental.pallas import tpu as pltpu
from jax.sharding import PartitionSpec as P

PARTS = 4


def translate_kernel(targets, slots, classes, points, row_ref, kind_ref, table_ref, ops_ref, out_ref, sums, ops,
                     even, odd, sems):
    part = points // PARTS
    columns = -(-classes // 128) * 128
    depth = even.shape[0]

    def fetch(p):
        piece = pl.ds(p * part, part)
        return pltpu.make_async_copy(ops_ref.at[piece], ops.at[piece], sems.at[p])

    for p in range(PARTS):
        fetch(p).start()

    def gather(t, chosen):
        for e in range(slots):
            chosen[e] = table_ref[row_ref[e * targets + t]]

    def sum_classes(t, chosen):
        flat = chosen.reshape(2 * depth, 128)
        low = flat[pl.ds(0, depth, stride=2), :].T
        high = flat[pl.ds(1, depth, stride=2), :].T
        left = jnp.concatenate([low, high[: points - 128]], axis=0).astype(jnp.bfloat16)
        kinds = kind_ref[pl.ds(t, 1), :]
        wanted = lax.broadcasted_iota(jnp.int32, (columns, depth), 0)
        onehot = jnp.where(kinds == wanted, 1.0, 0.0).astype(jnp.bfloat16)
        total = lax.dot_general(left, onehot, (((1,), (1,)), ((), ())), preferred_element_type=jnp.float32)
        for l in range(columns // 128):
            sums[pl.ds(l * points * targets + t, points, stride=targets), :] = total[:, 128 * l: 128 * l + 128]

    for chosen in (even, odd):
        chosen[pl.ds(slots, depth - slots)] = jnp.zeros((depth - slots, 2, 128), jnp.float32)
    gather(0, even)

    def pair(h, _):
        t = 2 * h
        gather(t + 1, odd)
        sum_classes(t, even)
        gather(lax.min(t + 2, targets - 1), even)
        sum_classes(t + 1, odd)
        return 0

    lax.fori_loop(0, targets // 2, pair, 0)

    for p in range(PARTS):
        fetch(p).wait()

    def multiply(i, total):
        left = jnp.concatenate(
            [sums[pl.ds(pl.multiple_of((l * points + i) * targets, 8), targets), :].astype(jnp.bfloat16)
             for l in range(columns // 128)], axis=1)[:, :classes]
        return total + lax.dot_general(left, ops[i], (((1,), (1,)), ((), ())), preferred_element_type=jnp.float32)

    out_ref[...] = lax.fori_loop(0, points, multiply, jnp.zeros((targets, points), jnp.float32), unroll=4)


def translate(table, entry_row, entry_class, entry_count, m2l_ops):
    targets, slots = entry_row.shape
    classes, points, _ = m2l_ops.shape
    depth = -(-slots // 64) * 64
    columns = -(-classes // 128) * 128
    live = lax.broadcasted_iota(jnp.int32, entry_row.shape, 1) < entry_count[:, None]
    kinds = jnp.pad(jnp.where(live, entry_class, -1), ((0, 0), (0, depth - slots)), constant_values=-1)
    smem = pl.BlockSpec(memory_space=pltpu.SMEM)
    vmem = pl.BlockSpec(memory_space=pltpu.VMEM)
    return pl.pallas_call(
        functools.partial(translate_kernel, targets, slots, classes, points),
        out_shape=jax.ShapeDtypeStruct((targets, points), jnp.float32),
        in_specs=[smem, vmem, vmem, pl.BlockSpec(memory_space=pl.ANY)],
        out_specs=vmem,
        scratch_shapes=[
            pltpu.VMEM((columns // 128 * points * targets, 128), jnp.float32),
            pltpu.VMEM((points, points, classes), jnp.bfloat16),
            pltpu.VMEM((depth, 2, 128), jnp.float32),
            pltpu.VMEM((depth, 2, 128), jnp.float32),
            pltpu.SemaphoreType.DMA((PARTS,)),
        ],
        compiler_params=pltpu.CompilerParams(vmem_limit_bytes=62 * 2**20),
    )(entry_row.T.reshape(-1), kinds, table, m2l_ops.transpose(1, 2, 0))


def body(
    fine_mult,
    m2m_ops,
    m2l_ops,
    check_to_equiv,
    l2l_ops,
    send_slots,
    fine_list,
    fine_class,
    fine_count,
    parent_list,
    parent_class,
    parent_count,
):
    cell_total, points = fine_mult.shape
    peer_count = send_slots.shape[1]
    capacity = send_slots.shape[2]
    wanted = lax.broadcasted_iota(jnp.int32, (1, cell_total), 1)
    onehot = (send_slots[0].reshape(-1, 1) == wanted).astype(jnp.bfloat16)
    outgoing = jnp.dot(onehot, fine_mult, preferred_element_type=jnp.float32).astype(jnp.bfloat16)
    outgoing = outgoing.reshape(peer_count, capacity, points)
    received = lax.all_to_all(outgoing, ("leaf", "sub"), split_axis=0, concat_axis=0, tiled=True)
    received = received.reshape(peer_count * capacity, points)
    children = fine_mult.reshape(cell_total // 8, 8, points)
    parent_mult = jnp.einsum(
        "pkq,kqr->pr", children, m2m_ops, preferred_element_type=jnp.float32
    ).astype(jnp.bfloat16)
    block_parents = lax.all_gather(parent_mult, "sub", axis=0, tiled=True)
    table = jnp.concatenate([fine_mult, received, block_parents], axis=0).astype(jnp.float32)
    table = jnp.pad(table, ((0, 0), (0, 256 - points))).reshape(-1, 2, 128)
    parent_first = cell_total + peer_count * capacity
    check = translate(
        table,
        jnp.concatenate([fine_list, parent_list + parent_first], axis=0),
        jnp.concatenate([fine_class, parent_class], axis=0),
        jnp.concatenate([fine_count, parent_count], axis=0),
        m2l_ops,
    )
    fine_check, parent_check = check[:cell_total], 0.5 * check[cell_total:]
    parent_local = jnp.dot(
        parent_check,
        check_to_equiv,
        precision=lax.Precision.HIGHEST,
        preferred_element_type=jnp.float32,
    ).astype(jnp.bfloat16)
    downward = jnp.einsum("pq,kqr->pkr", parent_local, l2l_ops, preferred_element_type=jnp.float32)
    return fine_check + downward.reshape(cell_total, points)


def solution(mesh):
    in_specs = (
        P(("leaf", "sub"), None),
        P(),
        P(),
        P(),
        P(),
        P(("leaf", "sub"), None, None),
        P(("leaf", "sub"), None),
        P(("leaf", "sub"), None),
        P(("leaf", "sub")),
        P(("leaf", "sub"), None),
        P(("leaf", "sub"), None),
        P(("leaf", "sub")),
    )
    out_specs = P(("leaf", "sub"), None)
    return jax.shard_map(body, mesh=mesh, in_specs=in_specs, out_specs=out_specs, check_vma=False)
```

time: 212 us -> 115 us (0.54); the launches traced: 209 us -> 114 us
  local copies, waits for them, and re-layouts: 113 us -> 7.94 us
  Pallas kernels: 0 us -> 69.6 us
  matrix products: 62.9 us -> 2.68 us
  waiting for transfers between devices: 0.01 us -> 18.4 us
  other arithmetic: 17.9 us -> 2.59 us
    gather x4 -> x0, local copies, waits for them, and re-layouts: 89.7 us -> none  [the longest x3 80.7 us: translate_block(): gathered = jnp.take(source_table, chosen.reshape(-1), axis=0, mode='clip')]
    pallas_call x0 -> x1, Pallas kernels: none -> 69.6 us  [translate(): pl.pallas_call(functools.partial(translate_kernel, targets, slots, classe...]
    dot_general x6 -> x1, matrix products: 62.3 us -> 1.37 us  [body(): jnp.dot(onehot, fine_mult, preferred_element_type=jnp.float32)]
    all_to_all x1, waiting for transfers between devices: 0.01 us -> 18.4 us  [body(): lax.all_to_all(outgoing, ('leaf', 'sub'), split_axis=0, concat_axis=0, ti...]
    and x2 -> x0, other arithmetic: 15.7 us -> none  [translate_block(): (kinds[:, None, :] == class_range) & active_slot[:, None, :]]
    reshape x6 -> x3, local copies, waits for them, and re-layouts: 19.2 us -> 4.34 us  [the longest x1 2.25 us: body(): table = jnp.pad(table, ((0, 0), (0, 256 - points))).reshape(-1, 2, 128)]
  transfers between devices with their start and end apart: 1 -> 1, of which waited for: 0 -> 1; matrix products, arithmetic and copies ran while one was open for 15% -> 2% of each run, Pallas kernels for 0% -> 0%
where the time goes in v2:
time: 115 us; the launch traced here: 114 us
  Pallas kernels  69.6 us (61%)
  waiting for transfers between devices  18.4 us (16%)
  local copies, waits for them, and re-layouts  7.94 us (7%)
  starting transfers between devices  7.3 us (6%)
  blocking collectives  5.59 us (5%)
  matrix products  2.68 us (2%)
  other arithmetic  2.59 us (2%)
    pallas_call x1, Pallas kernels, translate(): pl.pallas_call(functools.partial(translate_kernel, targets, slots, classe...  69.6 us
    all_to_all x1, waiting for transfers between devices, body(): lax.all_to_all(outgoing, ('leaf', 'sub'), split_axis=0, concat_axis=0, ti...  18.4 us
    all_to_all x1, starting transfers between devices, body(): lax.all_to_all(outgoing, ('leaf', 'sub'), split_axis=0, concat_axis=0, ti...  7.3 us
    all_gather x1, blocking collectives, body(): block_parents = lax.all_gather(parent_mult, 'sub', axis=0, tiled=True)  5.59 us
  transfers between devices with their start and end apart: 1, of which 1 were waited for; matrix products, arithmetic and copies ran while one was open for 2% of the time, Pallas kernels for 0%

profile of v2, /device:TPU:0, one launch (start us, length us, event | category | flops | bytes accessed | tf_op | source)
XLA Modules:
  0.0 114.3 jit_solution(2655807836965027129)
XLA Ops:
  0.0 0.0 copy-start
  0.0 0.0 copy-start.4
  0.0 0.0 copy-start.5
  0.0 0.9 eq.15
  0.9 0.0 copy-start.8
  0.9 0.0 copy-start.6
  0.9 1.4 %convolution_convert_fusion = bf16[2048,152]{0,1:T(8,128)(2,1)S(1)} fusion(bf16[128,152]{0,1:T(8,128)(2,1)} %param.12, s32[2048]{0:T(1024)S(1)} %eq.15), kind=kOutput, calls=%fused_computation | convolution fusion | flops 80265216 | bytes 669696 | tf_op jit(solution)/shard_map/dot_general | solution.py:112
  2.2 0.0 copy-start.9
  2.3 0.0 copy-start.10
  2.3 0.0 copy-start.7
  2.3 1.3 %copy.56 = bf16[2048,152]{1,0:T(8,128)(2,1)} copy(bf16[2048,152]{0,1:T(8,128)(2,1)S(1)} %convolution_convert_fusion) | data formatting | bytes 1245184 | tf_op jit(solution)/shard_map/reshape | solution.py:113
  3.6 0.0 copy-start.2
  3.6 7.3 %all-to-all-start = ((bf16[32,64,152]{2,1,0:T(8,128)(2,1)}), bf16[32,64,152]{2,1,0:T(8,128)(2,1)S(1)}, u32[]{:S(2)}, u32[]{:S(2)}) async-start(bf16[32,64,152]{2,1,0:T(8,128)(2,1)} %bitcast.1), calls=%async_computation | async-start | bytes 2097152 | tf_op jit(solution)/shard_map/all_to_all | solution.py:114
  10.9 0.0 copy-done.4
  10.9 0.1 copy.52
  11.0 0.0 copy-done.5
  11.0 0.1 copy.47
  11.1 0.0 copy-done.8
  11.1 0.1 copy.46
  11.2 0.0 copy-done.6
  11.3 0.8 reshape.22.row_ref
  12.1 0.0 copy-done.9
  12.1 0.0 copy-done.10
  12.1 0.0 copy-done.7
  12.1 0.1 add_select_fusion
  12.2 0.7 pad.9.kind_ref
  12.9 0.0 copy-done.2
  12.9 0.2 fusion.6
  13.1 5.6 %all_gather.3 = bf16[64,152]{1,0:T(8,128)(2,1)S(1)} all-gather(bf16[16,152]{1,0:T(8,128)(2,1)S(1)} %fusion.6), channel_id=1, replica_groups=mesh['leaf'=8,'sub'=4] {'sub'}, dimensions={0}, use_global_device_ids=true | all-gather | bytes 24320 | tf_op jit(solution)/shard_map/all_gather | solution.py:120
  18.7 18.4 %all-to-all-done = bf16[32,64,152]{2,1,0:T(8,128)(2,1)S(1)} async-done(((bf16[32,64,152]{2,1,0:T(8,128)(2,1)}), bf16[32,64,152]{2,1,0:T(8,128)(2,1)S(1)}, u32[]{:S(2)}, u32[]{:S(2)}) %all-to-all-start) | async-done | bytes 622624 | tf_op jit(solution)/shard_map/all_to_all | solution.py:114
  37.1 0.0 copy-start.1
  37.1 1.0 copy-done.1
  38.1 1.5 %fusion.5 = f32[2240,256]{1,0:T(8,128)S(1)} fusion(bf16[64,152]{1,0:T(8,128)(2,1)S(1)} %all_gather.3, bf16[2048,152]{1,0:T(8,128)(2,1)} %bitcast.20, bf16[128,152]{1,0:T(8,128)(2,1)S(1)} %copy.52), kind=kLoop, calls=%fused_computation.7 | loop fusion | flops 5734400 | bytes 2974720 | tf_op jit(solution)/shard_map/reshape | solution.py:122
  39.6 2.2 %reshape.30.table_ref = f32[2240,2,128]{2,1,0:T(2,128)} reshape(f32[2240,256]{1,0:T(8,128)S(1)} %fusion.5) | data formatting | bytes 4587520 | tf_op jit(solution)/shard_map/reshape | solution.py:122
  41.8 0.0 copy-start.3
  41.8 69.6 %shard_map.118 = f32[144,152]{1,0:T(8,128)} custom-call(s32[27216]{0:T(1024)} %reshape.22.row_ref, s32[144,192]{1,0:T(8,128)} %pad.9.kind_ref, f32[2240,2,128]{2,1,0:T(2,128)} %reshape.30.table_ref, bf16[152,152,316]{2,1,0:T(8,128)(2,1)} %bitcast.19), custom_call_target="tpu_custom_call" | custom-call | tf_op jit(solution)/shard_map/pallas_call | solution.py:77
  111.4 0.0 copy-done.3
  111.5 0.9 fusion.7
  112.3 0.0 copy-done
  112.4 0.2 fusion.12
  112.6 1.0 slice_add_fusion
  113.6 0.7 copy.55
  (3 shorter events, 0.0 us)
Async XLA Ops:
  0.0 112.4 %copy-start = (bf16[8,152,152]{2,1,0:T(8,128)(2,1)S(1)}, bf16[8,152,152]{2,1,0:T(8,128)(2,1)}, u32[]{:S(2)}) copy-start(bf16[8,152,152]{2,1,0:T(8,128)(2,1)} %param.16) | copy-start | bytes 1108996
  0.0 10.9 %copy-start.4 = (bf16[128,152]{0,1:T(8,128)(2,1)S(1)}, bf16[128,152]{0,1:T(8,128)(2,1)}, u32[]{:S(2)}) copy-start(bf16[128,152]{0,1:T(8,128)(2,1)} %param.12) | copy-start | bytes 116740
  0.0 11.0 %copy-start.5 = (s32[128,189]{0,1:T(8,128)S(1)}, s32[128,189]{0,1:T(8,128)}, u32[]{:S(2)}) copy-start(s32[128,189]{0,1:T(8,128)} %param.19) | copy-start | bytes 290308
  0.9 10.3 %copy-start.8 = (s32[16,189]{1,0:T(8,128)S(1)}, s32[16,189]{1,0:T(8,128)}, u32[]{:S(2)}) copy-start(s32[16,189]{1,0:T(8,128)} %param.21) | copy-start | bytes 36292
  0.9 10.4 %copy-start.6 = (s32[128,189]{0,1:T(8,128)S(1)}, s32[128,189]{0,1:T(8,128)}, u32[]{:S(2)}) copy-start(s32[128,189]{0,1:T(8,128)} %param.18) | copy-start | bytes 290308
  2.2 9.8 %copy-start.9 = (s32[16]{0:T(128)S(1)}, s32[16]{0:T(128)}, u32[]{:S(2)}) copy-start(s32[16]{0:T(128)} %param.23) | copy-start | bytes 196
  2.3 9.8 %copy-start.10 = (s32[128]{0:T(128)S(1)}, s32[128]{0:T(128)}, u32[]{:S(2)}) copy-start(s32[128]{0:T(128)} %param.20) | copy-start | bytes 1540
  2.3 9.8 %copy-start.7 = (s32[16,189]{1,0:T(8,128)S(1)}, s32[16,189]{1,0:T(8,128)}, u32[]{:S(2)}) copy-start(s32[16,189]{1,0:T(8,128)} %param.22) | copy-start | bytes 36292
  3.6 9.3 %copy-start.2 = (bf16[8,152,152]{2,1,0:T(8,128)(2,1)S(1)}, bf16[8,152,152]{2,1,0:T(8,128)(2,1)}, u32[]{:S(2)}) copy-start(bf16[8,152,152]{2,1,0:T(8,128)(2,1)} %param.13) | copy-start | bytes 1108996
  3.6 33.5 %all-to-all-start = ((bf16[32,64,152]{2,1,0:T(8,128)(2,1)}), bf16[32,64,152]{2,1,0:T(8,128)(2,1)S(1)}, u32[]{:S(2)}, u32[]{:S(2)}) async-start(bf16[32,64,152]{2,1,0:T(8,128)(2,1)} %bitcast.1), calls=%async_computation | async-start | bytes 2097152 | tf_op jit(solution)/shard_map/all_to_all | solution.py:114
  37.1 1.0 copy-start.1
  41.8 69.6 %copy-start.3 = (f32[152,152]{1,0:T(8,128)S(1)}, f32[152,152]{1,0:T(8,128)}, u32[]{:S(2)}) copy-start(f32[152,152]{1,0:T(8,128)} %param.15) | copy-start | bytes 277252

commit v3 on v2

--- a/solution.py
+++ b/solution.py
@@ -8,13 +8,16 @@
 from jax.sharding import PartitionSpec as P
 
 PARTS = 4
+BATCH = 4
+EXTRA = 1
 
 
 def translate_kernel(targets, slots, classes, points, row_ref, kind_ref, table_ref, ops_ref, out_ref, sums, ops,
                      even, odd, sems):
     part = points // PARTS
     columns = -(-classes // 128) * 128
-    depth = even.shape[0]
+    depth = even.shape[0] // BATCH
+    pitch = targets + EXTRA
 
     def fetch(p):
         piece = pl.ds(p * part, part)
@@ -23,42 +26,49 @@
     for p in range(PARTS):
         fetch(p).start()
 
-    def gather(t, chosen):
+    def gather(t, u, chosen):
         for e in range(slots):
-            chosen[e] = table_ref[row_ref[e * targets + t]]
+            chosen[u * depth + e] = table_ref[row_ref[e * targets + t]]
 
-    def sum_classes(t, chosen):
-        flat = chosen.reshape(2 * depth, 128)
-        low = flat[pl.ds(0, depth, stride=2), :].T
-        high = flat[pl.ds(1, depth, stride=2), :].T
-        left = jnp.concatenate([low, high[: points - 128]], axis=0).astype(jnp.bfloat16)
+    def class_sums(t, u, chosen):
+        flat = chosen.reshape(2 * BATCH * depth, 128)
+        low = flat[pl.ds(2 * u * depth, depth, stride=2), :].astype(jnp.bfloat16)
+        high = flat[pl.ds(2 * u * depth + 1, depth, stride=2), :].astype(jnp.bfloat16)
+        left = jnp.concatenate([low, high], axis=1)[:, :points].T
         kinds = kind_ref[pl.ds(t, 1), :]
         wanted = lax.broadcasted_iota(jnp.int32, (columns, depth), 0)
         onehot = jnp.where(kinds == wanted, 1.0, 0.0).astype(jnp.bfloat16)
-        total = lax.dot_general(left, onehot, (((1,), (1,)), ((), ())), preferred_element_type=jnp.float32)
+        return lax.dot_general(left, onehot, (((1,), (1,)), ((), ())), preferred_element_type=jnp.float32)
+
+    def keep(t, total):
         for l in range(columns // 128):
-            sums[pl.ds(l * points * targets + t, points, stride=targets), :] = total[:, 128 * l: 128 * l + 128]
+            sums[pl.ds(l * points * pitch + t, points, stride=pitch), :] = total[:, 128 * l: 128 * l + 128]
 
     for chosen in (even, odd):
-        chosen[pl.ds(slots, depth - slots)] = jnp.zeros((depth - slots, 2, 128), jnp.float32)
-    gather(0, even)
+        for u in range(BATCH):
+            chosen[pl.ds(u * depth + slots, depth - slots)] = jnp.zeros((depth - slots, 2, 128), jnp.float32)
+    for u in range(BATCH):
+        gather(u, u, even)
 
     def pair(h, _):
-        t = 2 * h
-        gather(t + 1, odd)
-        sum_classes(t, even)
-        gather(lax.min(t + 2, targets - 1), even)
-        sum_classes(t + 1, odd)
+        first = 2 * BATCH * h
+        for now, later in ((even, odd), (odd, even)):
+            following = lax.min(first + BATCH, targets - BATCH)
+            for u in range(BATCH):
+                total = class_sums(first + u, u, now)
+                gather(following + u, u, later)
+                keep(first + u, total)
+            first += BATCH
         return 0
 
-    lax.fori_loop(0, targets // 2, pair, 0)
+    lax.fori_loop(0, targets // (2 * BATCH), pair, 0)
 
     for p in range(PARTS):
         fetch(p).wait()
 
     def multiply(i, total):
         left = jnp.concatenate(
-            [sums[pl.ds(pl.multiple_of((l * points + i) * targets, 8), targets), :].astype(jnp.bfloat16)
+            [sums[pl.ds((l * points + i) * pitch, targets), :].astype(jnp.bfloat16)
              for l in range(columns // 128)], axis=1)[:, :classes]
         return total + lax.dot_general(left, ops[i], (((1,), (1,)), ((), ())), preferred_element_type=jnp.float32)
 
@@ -80,10 +90,10 @@
         in_specs=[smem, vmem, vmem, pl.BlockSpec(memory_space=pl.ANY)],
         out_specs=vmem,
         scratch_shapes=[
-            pltpu.VMEM((columns // 128 * points * targets, 128), jnp.float32),
+            pltpu.VMEM((columns // 128 * points * (targets + EXTRA), 128), jnp.float32),
             pltpu.VMEM((points, points, classes), jnp.bfloat16),
-            pltpu.VMEM((depth, 2, 128), jnp.float32),
-            pltpu.VMEM((depth, 2, 128), jnp.float32),
+            pltpu.VMEM((BATCH * depth, 2, 128), jnp.float32),
+            pltpu.VMEM((BATCH * depth, 2, 128), jnp.float32),
             pltpu.SemaphoreType.DMA((PARTS,)),
         ],
         compiler_params=pltpu.CompilerParams(vmem_limit_bytes=62 * 2**20),

time: 115 us -> 98.7 us (0.86)
  Pallas kernels: 69.6 us -> 53.6 us
    pallas_call x1, Pallas kernels: 69.6 us -> 53.6 us  [translate(): pl.pallas_call(functools.partial(translate_kernel, targets, slots, classe...]
where the time goes in v3:
time: 98.7 us; the launch traced here: 98.3 us
  Pallas kernels  53.6 us (54%)
  waiting for transfers between devices  18.4 us (19%)
  local copies, waits for them, and re-layouts  7.94 us (8%)
  starting transfers between devices  7.3 us (7%)
  blocking collectives  5.59 us (6%)
  matrix products  2.68 us (3%)
  other arithmetic  2.59 us (3%)
    pallas_call x1, Pallas kernels, translate(): pl.pallas_call(functools.partial(translate_kernel, targets, slots, classe...  53.6 us
    all_to_all x1, waiting for transfers between devices, body(): lax.all_to_all(outgoing, ('leaf', 'sub'), split_axis=0, concat_axis=0, ti...  18.4 us
    all_to_all x1, starting transfers between devices, body(): lax.all_to_all(outgoing, ('leaf', 'sub'), split_axis=0, concat_axis=0, ti...  7.3 us
    all_gather x1, blocking collectives, body(): block_parents = lax.all_gather(parent_mult, 'sub', axis=0, tiled=True)  5.59 us
    reshape x1, local copies, waits for them, and re-layouts, body(): table = jnp.pad(table, ((0, 0), (0, 256 - points))).reshape(-1, 2, 128)  2.25 us
  transfers between devices with their start and end apart: 1, of which 1 were waited for; matrix products, arithmetic and copies ran while one was open for 2% of the time, Pallas kernels for 0%

profile of v3, /device:TPU:0, one launch (start us, length us, event | category | flops | bytes accessed | tf_op | source)
XLA Modules:
  0.0 98.3 jit_solution(12787339351187950436)
XLA Ops:
  0.0 0.0 copy-start
  0.0 0.0 copy-start.4
  0.0 0.0 copy-start.5
  0.0 0.9 eq.15
  0.9 0.0 copy-start.8
  0.9 0.0 copy-start.6
  0.9 1.4 %convolution_convert_fusion = bf16[2048,152]{0,1:T(8,128)(2,1)S(1)} fusion(bf16[128,152]{0,1:T(8,128)(2,1)} %param.12, s32[2048]{0:T(1024)S(1)} %eq.15), kind=kOutput, calls=%fused_computation | convolution fusion | flops 80265216 | bytes 669696 | tf_op jit(solution)/shard_map/dot_general | solution.py:122
  2.2 0.0 copy-start.9
  2.3 0.0 copy-start.10
  2.3 0.0 copy-start.7
  2.3 1.3 %copy.56 = bf16[2048,152]{1,0:T(8,128)(2,1)} copy(bf16[2048,152]{0,1:T(8,128)(2,1)S(1)} %convolution_convert_fusion) | data formatting | bytes 1245184 | tf_op jit(solution)/shard_map/reshape | solution.py:123
  3.6 0.0 copy-start.2
  3.6 7.3 %all-to-all-start = ((bf16[32,64,152]{2,1,0:T(8,128)(2,1)}), bf16[32,64,152]{2,1,0:T(8,128)(2,1)S(1)}, u32[]{:S(2)}, u32[]{:S(2)}) async-start(bf16[32,64,152]{2,1,0:T(8,128)(2,1)} %bitcast.1), calls=%async_computation | async-start | bytes 2097152 | tf_op jit(solution)/shard_map/all_to_all | solution.py:124
  10.9 0.0 copy-done.4
  10.9 0.1 copy.52
  11.0 0.0 copy-done.5
  11.0 0.1 copy.47
  11.1 0.0 copy-done.8
  11.1 0.1 copy.46
  11.2 0.0 copy-done.6
  11.3 0.8 reshape.22.row_ref
  12.1 0.0 copy-done.9
  12.1 0.0 copy-done.10
  12.1 0.0 copy-done.7
  12.1 0.1 add_select_fusion
  12.2 0.7 pad.9.kind_ref
  12.9 0.0 copy-done.2
  12.9 0.2 fusion.6
  13.1 5.6 %all_gather.3 = bf16[64,152]{1,0:T(8,128)(2,1)S(1)} all-gather(bf16[16,152]{1,0:T(8,128)(2,1)S(1)} %fusion.6), channel_id=1, replica_groups=mesh['leaf'=8,'sub'=4] {'sub'}, dimensions={0}, use_global_device_ids=true | all-gather | bytes 24320 | tf_op jit(solution)/shard_map/all_gather | solution.py:130
  18.7 18.4 %all-to-all-done = bf16[32,64,152]{2,1,0:T(8,128)(2,1)S(1)} async-done(((bf16[32,64,152]{2,1,0:T(8,128)(2,1)}), bf16[32,64,152]{2,1,0:T(8,128)(2,1)S(1)}, u32[]{:S(2)}, u32[]{:S(2)}) %all-to-all-start) | async-done | bytes 622624 | tf_op jit(solution)/shard_map/all_to_all | solution.py:124
  37.1 0.0 copy-start.1
  37.1 1.0 copy-done.1
  38.1 1.5 %fusion.5 = f32[2240,256]{1,0:T(8,128)S(1)} fusion(bf16[64,152]{1,0:T(8,128)(2,1)S(1)} %all_gather.3, bf16[2048,152]{1,0:T(8,128)(2,1)} %bitcast.20, bf16[128,152]{1,0:T(8,128)(2,1)S(1)} %copy.52), kind=kLoop, calls=%fused_computation.7 | loop fusion | flops 5734400 | bytes 2974720 | tf_op jit(solution)/shard_map/reshape | solution.py:132
  39.6 2.2 %reshape.30.table_ref = f32[2240,2,128]{2,1,0:T(2,128)} reshape(f32[2240,256]{1,0:T(8,128)S(1)} %fusion.5) | data formatting | bytes 4587520 | tf_op jit(solution)/shard_map/reshape | solution.py:132
  41.8 0.0 copy-start.3
  41.8 53.6 %shard_map.118 = f32[144,152]{1,0:T(8,128)} custom-call(s32[27216]{0:T(1024)} %reshape.22.row_ref, s32[144,192]{1,0:T(8,128)} %pad.9.kind_ref, f32[2240,2,128]{2,1,0:T(2,128)} %reshape.30.table_ref, bf16[152,152,316]{2,1,0:T(8,128)(2,1)} %bitcast.19), custom_call_target="tpu_custom_call" | custom-call | tf_op jit(solution)/shard_map/pallas_call | solution.py:87
  95.5 0.0 copy-done.3
  95.5 0.9 fusion.7
  96.3 0.0 copy-done
  96.4 0.2 fusion.12
  96.6 1.0 %slice_add_fusion = f32[128,152]{1,0:T(8,128)S(1)} fusion(f32[144,152]{1,0:T(8,128)} %shard_map.118, f32[16,8,152]{2,0,1:T(8,128)S(1)} %fusion.12), kind=kLoop, calls=%fused_computation.17 | loop fusion | flops 19456 | bytes 233472 | tf_op jit(solution)/shard_map/add | solution.py:149
  97.6 0.7 copy.55
  (3 shorter events, 0.0 us)
Async XLA Ops:
  0.0 96.4 %copy-start = (bf16[8,152,152]{2,1,0:T(8,128)(2,1)S(1)}, bf16[8,152,152]{2,1,0:T(8,128)(2,1)}, u32[]{:S(2)}) copy-start(bf16[8,152,152]{2,1,0:T(8,128)(2,1)} %param.16) | copy-start | bytes 1108996
  0.0 10.9 %copy-start.4 = (bf16[128,152]{0,1:T(8,128)(2,1)S(1)}, bf16[128,152]{0,1:T(8,128)(2,1)}, u32[]{:S(2)}) copy-start(bf16[128,152]{0,1:T(8,128)(2,1)} %param.12) | copy-start | bytes 116740
  0.0 11.0 %copy-start.5 = (s32[128,189]{0,1:T(8,128)S(1)}, s32[128,189]{0,1:T(8,128)}, u32[]{:S(2)}) copy-start(s32[128,189]{0,1:T(8,128)} %param.19) | copy-start | bytes 290308
  0.9 10.3 %copy-start.8 = (s32[16,189]{1,0:T(8,128)S(1)}, s32[16,189]{1,0:T(8,128)}, u32[]{:S(2)}) copy-start(s32[16,189]{1,0:T(8,128)} %param.21) | copy-start | bytes 36292
  0.9 10.4 %copy-start.6 = (s32[128,189]{0,1:T(8,128)S(1)}, s32[128,189]{0,1:T(8,128)}, u32[]{:S(2)}) copy-start(s32[128,189]{0,1:T(8,128)} %param.18) | copy-start | bytes 290308
  2.2 9.8 %copy-start.9 = (s32[16]{0:T(128)S(1)}, s32[16]{0:T(128)}, u32[]{:S(2)}) copy-start(s32[16]{0:T(128)} %param.23) | copy-start | bytes 196
  2.3 9.8 %copy-start.10 = (s32[128]{0:T(128)S(1)}, s32[128]{0:T(128)}, u32[]{:S(2)}) copy-start(s32[128]{0:T(128)} %param.20) | copy-start | bytes 1540
  2.3 9.8 %copy-start.7 = (s32[16,189]{1,0:T(8,128)S(1)}, s32[16,189]{1,0:T(8,128)}, u32[]{:S(2)}) copy-start(s32[16,189]{1,0:T(8,128)} %param.22) | copy-start | bytes 36292
  3.6 9.3 %copy-start.2 = (bf16[8,152,152]{2,1,0:T(8,128)(2,1)S(1)}, bf16[8,152,152]{2,1,0:T(8,128)(2,1)}, u32[]{:S(2)}) copy-start(bf16[8,152,152]{2,1,0:T(8,128)(2,1)} %param.13) | copy-start | bytes 1108996
  3.6 33.5 %all-to-all-start = ((bf16[32,64,152]{2,1,0:T(8,128)(2,1)}), bf16[32,64,152]{2,1,0:T(8,128)(2,1)S(1)}, u32[]{:S(2)}, u32[]{:S(2)}) async-start(bf16[32,64,152]{2,1,0:T(8,128)(2,1)} %bitcast.1), calls=%async_computation | async-start | bytes 2097152 | tf_op jit(solution)/shard_map/all_to_all | solution.py:124
  37.1 1.0 copy-start.1
  41.8 53.6 %copy-start.3 = (f32[152,152]{1,0:T(8,128)S(1)}, f32[152,152]{1,0:T(8,128)}, u32[]{:S(2)}) copy-start(f32[152,152]{1,0:T(8,128)} %param.15) | copy-start | bytes 277252

commit v4 on v3

--- a/solution.py
+++ b/solution.py
@@ -8,12 +8,80 @@
 from jax.sharding import PartitionSpec as P
 
 PARTS = 4
+FOLD = 4
 BATCH = 4
 EXTRA = 1
 
 
-def translate_kernel(targets, slots, classes, points, row_ref, kind_ref, table_ref, ops_ref, out_ref, sums, ops,
-                     even, odd, sems):
+def exchange_kernel(peers, subs, out_ref, mine_ref, received_ref, parents_ref, send_sems, recv_sems, parent_send,
+                    parent_recv, own_sems):
+    leaf, sub = lax.axis_index("leaf"), lax.axis_index("sub")
+    me = leaf * subs + sub
+    barrier = pltpu.get_barrier_semaphore()
+
+    def cells(o):
+        other = lax.rem(me + o, peers)
+        return pltpu.make_async_remote_copy(
+            src_ref=out_ref.at[other], dst_ref=received_ref.at[me], send_sem=send_sems.at[o], recv_sem=recv_sems.at[o],
+            device_id=(other // subs, lax.rem(other, subs)), device_id_type=pl.DeviceIdType.MESH)
+
+    def parents(o):
+        return pltpu.make_async_remote_copy(
+            src_ref=mine_ref, dst_ref=parents_ref.at[sub], send_sem=parent_send.at[o], recv_sem=parent_recv.at[o],
+            device_id=(leaf, lax.rem(sub + o, subs)), device_id_type=pl.DeviceIdType.MESH)
+
+    def greet(o, _):
+        other = lax.rem(me + o, peers)
+        pl.semaphore_signal(barrier, inc=1, device_id=(other // subs, lax.rem(other, subs)),
+                            device_id_type=pl.DeviceIdType.MESH)
+        return 0
+
+    lax.fori_loop(1, peers, greet, 0)
+    own = pltpu.make_async_copy(out_ref.at[me], received_ref.at[me], own_sems.at[0])
+    own_parents = pltpu.make_async_copy(mine_ref, parents_ref.at[sub], own_sems.at[1])
+    own.start()
+    own_parents.start()
+    pl.semaphore_wait(barrier, peers - 1)
+
+    def start(o, _):
+        cells(o).start()
+        return 0
+
+    def finish(o, _):
+        cells(o).wait()
+        return 0
+
+    lax.fori_loop(1, peers, start, 0)
+    for o in range(1, subs):
+        parents(o).start()
+    own.wait()
+    own_parents.wait()
+    for o in range(1, subs):
+        parents(o).wait()
+    lax.fori_loop(1, peers, finish, 0)
+
+
+def exchange(outgoing, mine, peers, subs):
+    vmem = pl.BlockSpec(memory_space=pltpu.VMEM)
+    return pl.pallas_call(
+        functools.partial(exchange_kernel, peers, subs),
+        out_shape=(jax.ShapeDtypeStruct(outgoing.shape, outgoing.dtype),
+                   jax.ShapeDtypeStruct((subs,) + mine.shape, mine.dtype)),
+        in_specs=[vmem, vmem],
+        out_specs=(vmem, vmem),
+        scratch_shapes=[
+            pltpu.SemaphoreType.DMA((peers,)),
+            pltpu.SemaphoreType.DMA((peers,)),
+            pltpu.SemaphoreType.DMA((subs,)),
+            pltpu.SemaphoreType.DMA((subs,)),
+            pltpu.SemaphoreType.DMA((2,)),
+        ],
+        compiler_params=pltpu.CompilerParams(collective_id=0, has_side_effects=True, vmem_limit_bytes=16 * 2**20),
+    )(outgoing, mine)
+
+
+def translate_kernel(targets, slots, classes, points, row_ref, kind_ref, mult_ref, received_ref, parents_ref, ops_ref,
+                     out_ref, table_ref, sums, ops, even, odd, sems):
     part = points // PARTS
     columns = -(-classes // 128) * 128
     depth = even.shape[0] // BATCH
@@ -25,6 +93,32 @@
 
     for p in range(PARTS):
         fetch(p).start()
+
+    cells = mult_ref.shape[0]
+    peers, packed, _ = received_ref.shape
+    subs, both, _ = parents_ref.shape
+    capacity, own = packed * FOLD // (FOLD + 1), both // 2
+    rest = points - 128
+    rows = table_ref.reshape(table_ref.shape[0] * 2, 128)
+    mult = mult_ref[...].astype(jnp.float32)
+    rows[pl.ds(0, cells, stride=2), :] = mult[:, :128]
+    rows[pl.ds(1, cells, stride=2), :] = jnp.concatenate(
+        [mult[:, 128:], jnp.zeros((cells, 128 - rest), jnp.float32)], axis=1)
+
+    def unpack(s, _):
+        first = 2 * (cells + s * capacity)
+        rows[pl.ds(first, capacity, stride=2), :] = received_ref[s, :capacity].astype(jnp.float32)
+        high = received_ref[s, capacity:].astype(jnp.float32)
+        for q in range(FOLD):
+            rows[pl.ds(first + 2 * q * (capacity // FOLD) + 1, capacity // FOLD, stride=2), :] = (
+                pltpu.roll(high, 128 - rest * q, 1) if q else high)
+        return 0
+
+    lax.fori_loop(0, peers, unpack, 0)
+    for s in range(subs):
+        first = 2 * (cells + peers * capacity + s * own)
+        rows[pl.ds(first, own, stride=2), :] = parents_ref[s, :own].astype(jnp.float32)
+        rows[pl.ds(first + 1, own, stride=2), :] = parents_ref[s, own:].astype(jnp.float32)
 
     def gather(t, u, chosen):
         for e in range(slots):
@@ -75,11 +169,13 @@
     out_ref[...] = lax.fori_loop(0, points, multiply, jnp.zeros((targets, points), jnp.float32), unroll=4)
 
 
-def translate(table, entry_row, entry_class, entry_count, m2l_ops):
+def translate(fine_mult, received, block_parents, entry_row, entry_class, entry_count, m2l_ops):
     targets, slots = entry_row.shape
     classes, points, _ = m2l_ops.shape
     depth = -(-slots // 64) * 64
     columns = -(-classes // 128) * 128
+    total_rows = fine_mult.shape[0] + received.shape[0] * received.shape[1] * FOLD // (FOLD + 1)
+    total_rows += block_parents.shape[0] * block_parents.shape[1] // 2
     live = lax.broadcasted_iota(jnp.int32, entry_row.shape, 1) < entry_count[:, None]
     kinds = jnp.pad(jnp.where(live, entry_class, -1), ((0, 0), (0, depth - slots)), constant_values=-1)
     smem = pl.BlockSpec(memory_space=pltpu.SMEM)
@@ -87,9 +183,10 @@
     return pl.pallas_call(
         functools.partial(translate_kernel, targets, slots, classes, points),
         out_shape=jax.ShapeDtypeStruct((targets, points), jnp.float32),
-        in_specs=[smem, vmem, vmem, pl.BlockSpec(memory_space=pl.ANY)],
+        in_specs=[smem, vmem, vmem, vmem, vmem, pl.BlockSpec(memory_space=pl.ANY)],
         out_specs=vmem,
         scratch_shapes=[
+            pltpu.VMEM((total_rows, 2, 128), jnp.float32),
             pltpu.VMEM((columns // 128 * points * (targets + EXTRA), 128), jnp.float32),
             pltpu.VMEM((points, points, classes), jnp.bfloat16),
             pltpu.VMEM((BATCH * depth, 2, 128), jnp.float32),
@@ -97,7 +194,7 @@
             pltpu.SemaphoreType.DMA((PARTS,)),
         ],
         compiler_params=pltpu.CompilerParams(vmem_limit_bytes=62 * 2**20),
-    )(entry_row.T.reshape(-1), kinds, table, m2l_ops.transpose(1, 2, 0))
+    )(entry_row.T.reshape(-1), kinds, fine_mult, received, block_parents, m2l_ops.transpose(1, 2, 0))
 
 
 def body(
@@ -117,22 +214,30 @@
     cell_total, points = fine_mult.shape
     peer_count = send_slots.shape[1]
     capacity = send_slots.shape[2]
-    wanted = lax.broadcasted_iota(jnp.int32, (1, cell_total), 1)
-    onehot = (send_slots[0].reshape(-1, 1) == wanted).astype(jnp.bfloat16)
-    outgoing = jnp.dot(onehot, fine_mult, preferred_element_type=jnp.float32).astype(jnp.bfloat16)
-    outgoing = outgoing.reshape(peer_count, capacity, points)
-    received = lax.all_to_all(outgoing, ("leaf", "sub"), split_axis=0, concat_axis=0, tiled=True)
-    received = received.reshape(peer_count * capacity, points)
+    subs = lax.axis_size("sub")
+    rest = points - 128
+    slots = send_slots[0].reshape(peer_count, FOLD, capacity // FOLD)
+    cell = lax.broadcasted_iota(jnp.int32, (1, 1, cell_total), 2)
+    onehot = (send_slots[0][:, :, None] == cell).astype(jnp.bfloat16).reshape(-1, cell_total)
+    low = jnp.dot(onehot, fine_mult[:, :128], preferred_element_type=jnp.float32).astype(jnp.bfloat16)
+    folded = jnp.concatenate([(slots[:, q, :, None] == cell).astype(jnp.bfloat16) for q in range(FOLD)], axis=2)
+    placed = jnp.concatenate(
+        [jnp.pad(fine_mult[:, 128:], ((0, 0), (rest * q, 128 - rest * (q + 1)))) for q in range(FOLD)], axis=0)
+    high = jnp.dot(folded.reshape(-1, FOLD * cell_total), placed,
+                   preferred_element_type=jnp.float32).astype(jnp.bfloat16)
+    outgoing = jnp.concatenate(
+        [low.reshape(peer_count, capacity, 128), high.reshape(peer_count, capacity // FOLD, 128)], axis=1)
     children = fine_mult.reshape(cell_total // 8, 8, points)
     parent_mult = jnp.einsum(
         "pkq,kqr->pr", children, m2m_ops, preferred_element_type=jnp.float32
     ).astype(jnp.bfloat16)
-    block_parents = lax.all_gather(parent_mult, "sub", axis=0, tiled=True)
-    table = jnp.concatenate([fine_mult, received, block_parents], axis=0).astype(jnp.float32)
-    table = jnp.pad(table, ((0, 0), (0, 256 - points))).reshape(-1, 2, 128)
+    mine = jnp.concatenate([parent_mult[:, :128], jnp.pad(parent_mult[:, 128:], ((0, 0), (0, 128 - rest)))], axis=0)
+    received, block_parents = exchange(outgoing, mine, peer_count, subs)
     parent_first = cell_total + peer_count * capacity
     check = translate(
-        table,
+        fine_mult,
+        received,
+        block_parents,
         jnp.concatenate([fine_list, parent_list + parent_first], axis=0),
         jnp.concatenate([fine_class, parent_class], axis=0),
         jnp.concatenate([fine_count, parent_count], axis=0),

time: 98.7 us -> 88.2 us (0.89)
  the two profiles are of different devices: /device:TPU:0 before, /device:TPU:15 now
where the time goes in v4:
time: 88.2 us; the launch traced here: 87.7 us
  Pallas kernels  77.1 us (87%)
  local copies, waits for them, and re-layouts  6.69 us (8%)
  matrix products  2.05 us (2%)
  other arithmetic  1.6 us (2%)
    pallas_call x1, Pallas kernels, translate(): pl.pallas_call(functools.partial(translate_kernel, targets, slots, classe...  56 us
    pallas_call x1, Pallas kernels, exchange(): pl.pallas_call(functools.partial(exchange_kernel, peers, subs), out_shape...  21.1 us
    unnamed x31, local copies, waits for them, and re-layouts  3 us

profile of v4, /device:TPU:15, one launch (start us, length us, event | category | flops | bytes accessed | tf_op | source)
XLA Modules:
  0.0 87.7 jit_solution(6316449566449141303)
XLA Ops:
  0.0 0.0 copy-start
  0.0 0.9 copy.21
  0.9 0.1 copy.24
  0.9 0.1 eq.92
  1.0 0.1 copy.25
  1.1 0.1 eq.96
  1.2 0.2 iota_compare_fusion.8
  1.4 0.1 copy.22
  1.5 0.1 eq.84
  1.6 0.1 copy.23
  1.6 0.1 eq.88
  1.7 0.2 iota_compare_fusion.10
  1.9 0.7 slice.38
  2.6 0.0 copy-start.9
  2.6 0.0 copy-start.5
  2.6 0.3 convolution_convert_fusion.1
  2.9 0.0 copy-start.3
  3.0 0.4 copy-done.9
  3.4 0.1 eq.80
  3.4 0.0 copy-done.5
  3.4 0.5 convolution_convert_fusion
  3.9 0.0 copy-start.7
  3.9 0.0 copy-start.12
  3.9 0.0 copy-start.13
  3.9 0.0 copy-start.10
  4.0 0.0 copy-start.11
  4.0 0.0 copy-start.8
  4.0 0.1 copy.28.mult_ref
  4.1 0.0 copy-start.4
  4.1 0.0 copy-done.3
  4.2 0.2 fusion
  4.4 21.1 %shard_map.118 = (bf16[32,80,128]{2,1,0:T(8,128)(2,1)S(1)}, bf16[4,32,128]{2,1,0:T(8,128)(2,1)S(1)}) custom-call(bf16[32,80,128]{2,1,0:T(8,128)(2,1)S(1)} %pad_maximum_fusion.out_ref, bf16[32,128]{1,0:T(8,128)(2,1)S(1)} %fusion.34.mine_ref), custom_call_target="tpu_custom_call" | custom-call | tf_op jit(solution)/shard_map/pallas_call | solution.py:66
  25.5 0.0 copy-start.1
  25.6 0.8 copy-done.1
  26.4 0.0 copy-start.2
  26.4 0.6 copy-done.2
  27.0 0.0 copy-done.7
  27.0 0.1 copy.20
  27.1 0.0 copy-done.12
  27.1 0.0 copy-done.13
  27.1 0.0 copy-done.10
  27.1 0.1 add_select_fusion
  27.2 0.7 pad.24.kind_ref
  27.9 0.0 copy-done.11
  27.9 0.1 copy.19
  28.0 0.0 copy-done.8
  28.1 0.0 copy-done.4
  28.1 0.8 reshape.37.row_ref
  28.8 0.0 copy-start.6
  28.9 56.0 %shard_map.119 = f32[144,152]{1,0:T(8,128)} custom-call(s32[27216]{0:T(1024)} %reshape.37.row_ref, s32[144,192]{1,0:T(8,128)} %pad.24.kind_ref, bf16[128,152]{1,0:T(8,128)(2,1)} %copy-done.4, bf16[32,80,128]{2,1,0:T(8,128)(2,1)} %copy-done.1, bf16[4,32,128]{2,1,0:T(8,128)(2,1)} %copy-done.2, bf16[152,152,316]{2,1,0:T(8,128)(2,1)} %bitcast.27), custom_call_target="tpu_custom_call" | custom-call | tf_op jit(solution)/shard_map/pallas_call | solution.py:183
  84.8 0.0 copy-done.6
  84.8 0.9 %fusion.1 = bf16[16,152,1]{1,0,2:T(8,128)(2,1)S(1)} fusion(f32[152,152]{1,0:T(8,128)S(1)} %copy-done.6, f32[144,152]{1,0:T(8,128)} %shard_map.119), kind=kOutput, calls=%fused_computation.5 | convolution fusion | flops 4440832 | bytes 113664 | tf_op jit(solution)/shard_map/dot_general | solution.py:247
  85.7 0.0 copy-done
  85.7 0.2 fusion.44
  85.9 1.0 %slice_add_fusion = f32[128,152]{1,0:T(8,128)S(1)} fusion(f32[144,152]{1,0:T(8,128)} %shard_map.119, f32[16,8,152]{2,0,1:T(8,128)S(1)} %fusion.44), kind=kLoop, calls=%fused_computation.38 | loop fusion | flops 19456 | bytes 233472 | tf_op jit(solution)/shard_map/add | solution.py:254
  86.9 0.7 copy.30
  (8 shorter events, 0.1 us)
Async XLA Ops:
  0.0 85.7 %copy-start = (bf16[8,152,152]{2,1,0:T(8,128)(2,1)S(1)}, bf16[8,152,152]{2,1,0:T(8,128)(2,1)}, u32[]{:S(2)}) copy-start(bf16[8,152,152]{2,1,0:T(8,128)(2,1)} %param.16) | copy-start | bytes 1108996
  2.6 0.7 copy-start.9
  2.6 0.8 copy-start.5
  2.9 1.2 %copy-start.3 = (bf16[8,152,152]{2,1,0:T(8,128)(2,1)S(1)}, bf16[8,152,152]{2,1,0:T(8,128)(2,1)}, u32[]{:S(2)}) copy-start(bf16[8,152,152]{2,1,0:T(8,128)(2,1)} %param.13) | copy-start | bytes 1108996
  3.9 23.1 %copy-start.7 = (s32[128,189]{0,1:T(8,128)S(1)}, s32[128,189]{0,1:T(8,128)}, u32[]{:S(2)}) copy-start(s32[128,189]{0,1:T(8,128)} %param.19) | copy-start | bytes 290308
  3.9 23.2 %copy-start.12 = (s32[16]{0:T(128)S(1)}, s32[16]{0:T(128)}, u32[]{:S(2)}) copy-start(s32[16]{0:T(128)} %param.23) | copy-start | bytes 196
  3.9 23.2 %copy-start.13 = (s32[128]{0:T(128)S(1)}, s32[128]{0:T(128)}, u32[]{:S(2)}) copy-start(s32[128]{0:T(128)} %param.20) | copy-start | bytes 1540
  3.9 23.2 %copy-start.10 = (s32[16,189]{1,0:T(8,128)S(1)}, s32[16,189]{1,0:T(8,128)}, u32[]{:S(2)}) copy-start(s32[16,189]{1,0:T(8,128)} %param.22) | copy-start | bytes 36292
  4.0 23.9 %copy-start.11 = (s32[16,189]{1,0:T(8,128)S(1)}, s32[16,189]{1,0:T(8,128)}, u32[]{:S(2)}) copy-start(s32[16,189]{1,0:T(8,128)} %param.21) | copy-start | bytes 36292
  4.0 24.0 %copy-start.8 = (s32[128,189]{0,1:T(8,128)S(1)}, s32[128,189]{0,1:T(8,128)}, u32[]{:S(2)}) copy-start(s32[128,189]{0,1:T(8,128)} %param.18) | copy-start | bytes 290308
  4.1 23.9 %copy-start.4 = (bf16[128,152]{1,0:T(8,128)(2,1)}, bf16[128,152]{1,0:T(8,128)(2,1)S(1)}, u32[]{:S(2)}) copy-start(bf16[128,152]{1,0:T(8,128)(2,1)S(1)} %copy.28.mult_ref) | copy-start | bytes 116740
  25.5 0.8 copy-start.1
  26.4 0.6 copy-start.2
  28.8 56.0 %copy-start.6 = (f32[152,152]{1,0:T(8,128)S(1)}, f32[152,152]{1,0:T(8,128)}, u32[]{:S(2)}) copy-start(f32[152,152]{1,0:T(8,128)} %param.15) | copy-start | bytes 277252

commit v5 on v4

--- a/solution.py
+++ b/solution.py
@@ -122,7 +122,9 @@
 
     def gather(t, u, chosen):
         for e in range(slots):
-            chosen[u * depth + e] = table_ref[row_ref[e * targets + t]]
+            place = 2 * (u * depth + e)
+            chosen.reshape(2 * BATCH * depth, 128)[place: place + 2, :] = (
+                rows[pl.ds(pl.multiple_of(row_ref[e * targets + t], 2), 2), :])
 
     def class_sums(t, u, chosen):
         flat = chosen.reshape(2 * BATCH * depth, 128)
@@ -166,7 +168,7 @@
              for l in range(columns // 128)], axis=1)[:, :classes]
         return total + lax.dot_general(left, ops[i], (((1,), (1,)), ((), ())), preferred_element_type=jnp.float32)
 
-    out_ref[...] = lax.fori_loop(0, points, multiply, jnp.zeros((targets, points), jnp.float32), unroll=4)
+    out_ref[...] = lax.fori_loop(0, points, multiply, jnp.zeros((targets, points), jnp.float32), unroll=8)
 
 
 def translate(fine_mult, received, block_parents, entry_row, entry_class, entry_count, m2l_ops):
@@ -194,7 +196,7 @@
             pltpu.SemaphoreType.DMA((PARTS,)),
         ],
         compiler_params=pltpu.CompilerParams(vmem_limit_bytes=62 * 2**20),
-    )(entry_row.T.reshape(-1), kinds, fine_mult, received, block_parents, m2l_ops.transpose(1, 2, 0))
+    )(2 * entry_row.T.reshape(-1), kinds, fine_mult, received, block_parents, m2l_ops.transpose(1, 2, 0))
 
 
 def body(

time: 88.2 us -> 78.7 us (0.89)
  Pallas kernels: 77.1 us -> 67.6 us
    pallas_call x1, Pallas kernels: 56 us -> 46.5 us  [translate(): pl.pallas_call(functools.partial(translate_kernel, targets, slots, classe...]
where the time goes in v5:
time: 78.7 us; the launch traced here: 78.2 us
  Pallas kernels  67.6 us (86%)
  local copies, waits for them, and re-layouts  6.69 us (9%)
  matrix products  2.05 us (3%)
  other arithmetic  1.6 us (2%)
    pallas_call x1, Pallas kernels, translate(): pl.pallas_call(functools.partial(translate_kernel, targets, slots, classe...  46.5 us
    pallas_call x1, Pallas kernels, exchange(): pl.pallas_call(functools.partial(exchange_kernel, peers, subs), out_shape...  21.1 us
    unnamed x31, local copies, waits for them, and re-layouts  3 us

profile of v5, /device:TPU:15, one launch (start us, length us, event | category | flops | bytes accessed | tf_op | source)
XLA Modules:
  0.0 78.2 jit_solution(12229994099643086095)
XLA Ops:
  0.0 0.0 copy-start
  0.0 0.9 %copy.21 = s32[1,32,64]{1,2,0:T(8,128)S(1)} copy(s32[1,32,64]{2,1,0:T(8,128)} %param.17) | data formatting | bytes 16384 | tf_op args[5]
  0.9 0.1 copy.24
  0.9 0.1 eq.92
  1.0 0.1 copy.25
  1.1 0.1 eq.96
  1.2 0.2 iota_compare_fusion.8
  1.4 0.1 copy.22
  1.5 0.1 eq.84
  1.6 0.1 copy.23
  1.6 0.1 eq.88
  1.7 0.2 iota_compare_fusion.10
  1.9 0.7 slice.38
  2.6 0.0 copy-start.9
  2.6 0.0 copy-start.5
  2.6 0.3 convolution_convert_fusion.1
  2.9 0.0 copy-start.3
  3.0 0.4 copy-done.9
  3.4 0.1 eq.80
  3.4 0.0 copy-done.5
  3.4 0.5 convolution_convert_fusion
  3.9 0.0 copy-start.7
  3.9 0.0 copy-start.12
  3.9 0.0 copy-start.13
  3.9 0.0 copy-start.10
  4.0 0.0 copy-start.11
  4.0 0.0 copy-start.8
  4.0 0.1 copy.28.mult_ref
  4.1 0.0 copy-start.4
  4.1 0.0 copy-done.3
  4.2 0.2 fusion
  4.4 21.1 %shard_map.118 = (bf16[32,80,128]{2,1,0:T(8,128)(2,1)S(1)}, bf16[4,32,128]{2,1,0:T(8,128)(2,1)S(1)}) custom-call(bf16[32,80,128]{2,1,0:T(8,128)(2,1)S(1)} %pad_maximum_fusion.out_ref, bf16[32,128]{1,0:T(8,128)(2,1)S(1)} %fusion.35.mine_ref), custom_call_target="tpu_custom_call" | custom-call | tf_op jit(solution)/shard_map/pallas_call | solution.py:66
  25.5 0.0 copy-start.1
  25.6 0.8 %copy-done.1 = bf16[32,80,128]{2,1,0:T(8,128)(2,1)} copy-done((bf16[32,80,128]{2,1,0:T(8,128)(2,1)}, bf16[32,80,128]{2,1,0:T(8,128)(2,1)S(1)}, u32[]{:S(2)}) %copy-start.1) | copy-done | bytes 655384
  26.4 0.0 copy-start.2
  26.4 0.6 copy-done.2
  27.0 0.0 copy-done.7
  27.0 0.1 copy.20
  27.1 0.0 copy-done.12
  27.1 0.0 copy-done.13
  27.1 0.0 copy-done.10
  27.1 0.1 add_select_fusion
  27.2 0.7 pad.24.kind_ref
  27.9 0.0 copy-done.11
  27.9 0.1 copy.19
  28.0 0.0 copy-done.8
  28.1 0.0 copy-done.4
  28.1 0.8 mul.19.row_ref
  28.9 0.0 copy-start.6
  28.9 46.5 %shard_map.119 = f32[144,152]{1,0:T(8,128)} custom-call(s32[27216]{0:T(1024)} %mul.19.row_ref, s32[144,192]{1,0:T(8,128)} %pad.24.kind_ref, bf16[128,152]{1,0:T(8,128)(2,1)} %copy-done.4, bf16[32,80,128]{2,1,0:T(8,128)(2,1)} %copy-done.1, bf16[4,32,128]{2,1,0:T(8,128)(2,1)} %copy-done.2, bf16[152,152,316]{2,1,0:T(8,128)(2,1)} %bitcast.27), custom_call_target="tpu_custom_call" | custom-call | tf_op jit(solution)/shard_map/pallas_call | solution.py:185
  75.4 0.0 copy-done.6
  75.4 0.9 %fusion.1 = bf16[16,152,1]{1,0,2:T(8,128)(2,1)S(1)} fusion(f32[152,152]{1,0:T(8,128)S(1)} %copy-done.6, f32[144,152]{1,0:T(8,128)} %shard_map.119), kind=kOutput, calls=%fused_computation.5 | convolution fusion | flops 4440832 | bytes 113664 | tf_op jit(solution)/shard_map/dot_general | solution.py:249
  76.2 0.0 copy-done
  76.3 0.2 fusion.45
  76.5 1.0 %slice_add_fusion = f32[128,152]{1,0:T(8,128)S(1)} fusion(f32[144,152]{1,0:T(8,128)} %shard_map.119, f32[16,8,152]{2,0,1:T(8,128)S(1)} %fusion.45), kind=kLoop, calls=%fused_computation.39 | loop fusion | flops 19456 | bytes 233472 | tf_op jit(solution)/shard_map/add | solution.py:256
  77.5 0.7 copy.30
  (8 shorter events, 0.1 us)
Async XLA Ops:
  0.0 76.3 %copy-start = (bf16[8,152,152]{2,1,0:T(8,128)(2,1)S(1)}, bf16[8,152,152]{2,1,0:T(8,128)(2,1)}, u32[]{:S(2)}) copy-start(bf16[8,152,152]{2,1,0:T(8,128)(2,1)} %param.16) | copy-start | bytes 1108996
  2.6 0.7 copy-start.9
  2.6 0.8 %copy-start.5 = (bf16[128,152]{0,1:T(8,128)(2,1)S(1)}, bf16[128,152]{0,1:T(8,128)(2,1)}, u32[]{:S(2)}) copy-start(bf16[128,152]{0,1:T(8,128)(2,1)} %param.12) | copy-start | bytes 116740
  2.9 1.2 %copy-start.3 = (bf16[8,152,152]{2,1,0:T(8,128)(2,1)S(1)}, bf16[8,152,152]{2,1,0:T(8,128)(2,1)}, u32[]{:S(2)}) copy-start(bf16[8,152,152]{2,1,0:T(8,128)(2,1)} %param.13) | copy-start | bytes 1108996
  3.9 23.1 %copy-start.7 = (s32[128,189]{0,1:T(8,128)S(1)}, s32[128,189]{0,1:T(8,128)}, u32[]{:S(2)}) copy-start(s32[128,189]{0,1:T(8,128)} %param.19) | copy-start | bytes 290308
  3.9 23.2 %copy-start.12 = (s32[16]{0:T(128)S(1)}, s32[16]{0:T(128)}, u32[]{:S(2)}) copy-start(s32[16]{0:T(128)} %param.23) | copy-start | bytes 196
  3.9 23.2 %copy-start.13 = (s32[128]{0:T(128)S(1)}, s32[128]{0:T(128)}, u32[]{:S(2)}) copy-start(s32[128]{0:T(128)} %param.20) | copy-start | bytes 1540
  3.9 23.2 %copy-start.10 = (s32[16,189]{1,0:T(8,128)S(1)}, s32[16,189]{1,0:T(8,128)}, u32[]{:S(2)}) copy-start(s32[16,189]{1,0:T(8,128)} %param.22) | copy-start | bytes 36292
  4.0 23.9 %copy-start.11 = (s32[16,189]{1,0:T(8,128)S(1)}, s32[16,189]{1,0:T(8,128)}, u32[]{:S(2)}) copy-start(s32[16,189]{1,0:T(8,128)} %param.21) | copy-start | bytes 36292
  4.0 24.0 %copy-start.8 = (s32[128,189]{0,1:T(8,128)S(1)}, s32[128,189]{0,1:T(8,128)}, u32[]{:S(2)}) copy-start(s32[128,189]{0,1:T(8,128)} %param.18) | copy-start | bytes 290308
  4.1 23.9 %copy-start.4 = (bf16[128,152]{1,0:T(8,128)(2,1)}, bf16[128,152]{1,0:T(8,128)(2,1)S(1)}, u32[]{:S(2)}) copy-start(bf16[128,152]{1,0:T(8,128)(2,1)S(1)} %copy.28.mult_ref) | copy-start | bytes 116740
  25.5 0.8 %copy-start.1 = (bf16[32,80,128]{2,1,0:T(8,128)(2,1)}, bf16[32,80,128]{2,1,0:T(8,128)(2,1)S(1)}, u32[]{:S(2)}) copy-start(bf16[32,80,128]{2,1,0:T(8,128)(2,1)S(1)} %get-tuple-element.7.received_ref) | copy-start | bytes 1966084
  26.4 0.6 copy-start.2
  28.9 46.5 %copy-start.6 = (f32[152,152]{1,0:T(8,128)S(1)}, f32[152,152]{1,0:T(8,128)}, u32[]{:S(2)}) copy-start(f32[152,152]{1,0:T(8,128)} %param.15) | copy-start | bytes 277252
